TPU v7x, 32 devices: a whole 2x2x4 slice. The times are simulated.
32 devices in a mesh: fsdp: 32 (over z, y, x, core).
Axes of the slice: x: 2, y: 2, z: 4, core: 2. Of those that a mesh axis runs over, the one named last changes fastest.
Arguments:
- tokens: bfloat16 [4096, 960], P('fsdp'), may hold values from -6 to 6
- cotangent: bfloat16 [4096, 960], P('fsdp'), may hold values from -6 to 6
- seq_lengths: int32 [64], replicated, may hold values from 16 to 112, as said below
- seq_owner: int32 [64], replicated, may hold values from 0 to 31, as said below
- query_weight: bfloat16 [921600], P('fsdp'), may hold values from -0.1875 to 0.1875
- key_weight: bfloat16 [307200], P('fsdp'), may hold values from -0.1875 to 0.1875
- value_weight: bfloat16 [307200], P('fsdp'), may hold values from -0.1875 to 0.1875
- out_weight: bfloat16 [921600], P('fsdp'), may hold values from -0.5 to 0.5
- gate_weight: bfloat16 [2457600], P('fsdp'), may hold values from -0.1875 to 0.1875
- up_weight: bfloat16 [2457600], P('fsdp'), may hold values from -0.1875 to 0.1875
- down_weight: bfloat16 [2457600], P('fsdp'), may hold values from -0.125 to 0.125
- attention_gain: float32 [960], replicated, may hold values from 0.5 to 1.5
- feedforward_gain: float32 [960], replicated, may hold values from 0.5 to 1.5
Outputs:
- layer_out: bfloat16 [4096, 960], P('fsdp')
- grad_tokens: bfloat16 [4096, 960], P('fsdp')
- grad_query_weight: float32 [921600], P('fsdp')
- grad_key_weight: float32 [307200], P('fsdp')
- grad_value_weight: float32 [307200], P('fsdp')
- grad_out_weight: float32 [921600], P('fsdp')
- grad_gate_weight: float32 [2457600], P('fsdp')
- grad_up_weight: float32 [2457600], P('fsdp')
- grad_down_weight: float32 [2457600], P('fsdp')
- grad_attention_gain: float32 [960], replicated
- grad_feedforward_gain: float32 [960], replicated
Inputs may be any that keep to these rules, and one draw needn't show every extreme that they name: `seq_lengths`: every device holds exactly two sequences, and the two lengths of a device sum to at most 128; some device is full in every draw. `seq_owner`: each device number appears exactly twice.
All inputs are finite; a program needn't handle non-finite values.
Results may differ from a plain program's by a relative error of at most 0.015.
Values may be sent and summed in bfloat16 or wider, within the bound.
A program may use at most 256 MiB of HBM per device.

v0:
```python
import math

import jax
import jax.numpy as jnp
from jax import lax
from jax.sharding import PartitionSpec as P

D = 960
HEADS = 15
KV_HEADS = 5
HD = 64
FF = 2560


EPSILON = 1e-05
ROPE_BASE = 10000.0
MASKED_SCORE = -1e30


def own_rows(seq_lengths, seq_owner, device, row_count):
    seq_count = seq_lengths.shape[0]
    seq_index = jnp.arange(seq_count, dtype=jnp.int32)
    is_mine = seq_owner == device
    first_seq = jnp.min(jnp.where(is_mine, seq_index, seq_count))
    second_seq = jnp.min(jnp.where(is_mine & (seq_index != first_seq), seq_index, seq_count))
    len_first = jnp.sum(jnp.where(seq_index == first_seq, seq_lengths, 0))
    len_second = jnp.sum(jnp.where(seq_index == second_seq, seq_lengths, 0))
    row_index = jnp.arange(row_count, dtype=jnp.int32)
    segment = (row_index >= len_first).astype(jnp.int32) + (
        row_index >= len_first + len_second
    ).astype(jnp.int32)
    seg_start = jnp.where(
        segment == 0, 0, jnp.where(segment == 1, len_first, len_first + len_second)
    )
    position = row_index - seg_start
    row_valid = (segment < 2).astype(jnp.float32)
    allowed = (segment[:, None] == segment[None, :]) & (row_index[None, :] <= row_index[:, None])
    return (position, row_valid, allowed)


def rope_tables(position, head_size):
    half_size = head_size // 2
    frequency = ROPE_BASE ** (-jnp.arange(half_size, dtype=jnp.float32) * 2.0 / head_size)
    angles = position.astype(jnp.float32)[:, None] * frequency[None, :]
    return (jnp.cos(angles), jnp.sin(angles))


def rotate(values, cosine, sine_table):
    half_size = values.shape[-1] // 2
    front_half = values[..., :half_size]
    back_half = values[..., half_size:]
    cos_part = cosine[:, None, :]
    sin_part = sine_table[:, None, :]
    return jnp.concatenate(
        [
            front_half * cos_part - back_half * sin_part,
            back_half * cos_part + front_half * sin_part,
        ],
        axis=-1,
    )


def unrotate(gradient, cosine, sine_table):
    half_size = gradient.shape[-1] // 2
    front_half = gradient[..., :half_size]
    back_half = gradient[..., half_size:]
    cos_part = cosine[:, None, :]
    sin_part = sine_table[:, None, :]
    return jnp.concatenate(
        [
            front_half * cos_part + back_half * sin_part,
            back_half * cos_part - front_half * sin_part,
        ],
        axis=-1,
    )


def rms_scale(values):
    return lax.rsqrt(jnp.mean(values * values, axis=-1, keepdims=True) + EPSILON)


def outer_sum(left_side, right_side):
    return lax.dot_general(
        left_side, right_side, (((0,), (0,)), ((), ())), preferred_element_type=jnp.float32
    )


def times_t(left_side, right_side):
    return lax.dot_general(
        left_side, right_side, (((1,), (1,)), ((), ())), preferred_element_type=jnp.float32
    )


def pack_shards(shard_list):
    return jnp.concatenate([piece.reshape(1, -1) for piece in shard_list], axis=1)


def unpack_gathered(whole, shard_list):
    result_list = []
    offset = 0
    for piece in shard_list:
        width = piece.shape[0]
        result_list.append(whole[:, offset : offset + width].reshape(-1))
        offset = offset + width
    return result_list


def pack_grads(grad_list, count):
    return jnp.concatenate([item.reshape(count, -1) for item in grad_list], axis=1)


def unpack_grads(summed, grad_list, count):
    result_list = []
    offset = 0
    for item in grad_list:
        width = item.size // count
        result_list.append(summed[:, offset : offset + width].reshape(-1))
        offset = offset + width
    return result_list


def shape_weights(flat_list):
    query_flat, key_flat, value_flat, out_flat, gate_flat, up_flat, down_flat = flat_list
    return (
        query_flat.reshape(D, HEADS * HD),
        key_flat.reshape(D, KV_HEADS * HD),
        value_flat.reshape(D, KV_HEADS * HD),
        out_flat.reshape(HEADS * HD, D),
        gate_flat.reshape(D, FF),
        up_flat.reshape(D, FF),
        down_flat.reshape(FF, D),
    )


def on_device(
    tokens,
    cotangent,
    seq_lengths,
    seq_owner,
    query_weight,
    key_weight,
    value_weight,
    out_weight,
    gate_weight,
    up_weight,
    down_weight,
    attention_gain,
    feedforward_gain,
):
    row_count = tokens.shape[0]
    groups = HEADS // KV_HEADS
    score_scale = 1.0 / math.sqrt(HD)
    count = lax.axis_size("fsdp")
    device = lax.axis_index("fsdp")
    position, row_valid, allowed = own_rows(seq_lengths, seq_owner, device, row_count)
    cosine, sine_table = rope_tables(position, HD)
    shard_list = (
        query_weight,
        key_weight,
        value_weight,
        out_weight,
        gate_weight,
        up_weight,
        down_weight,
    )
    gathered = lax.all_gather(pack_shards(shard_list), "fsdp", axis=0, tiled=True)
    w_query, w_key, w_value, w_out, w_gate, w_up, w_down = shape_weights(
        unpack_gathered(gathered, shard_list)
    )
    inputs = tokens.astype(jnp.float32)
    scale_one = rms_scale(inputs)
    normed_one = inputs * scale_one
    low_one = (normed_one * attention_gain).astype(jnp.bfloat16)
    query_pre = jnp.dot(low_one, w_query, preferred_element_type=jnp.float32).reshape(
        row_count, HEADS, HD
    )
    key_pre = jnp.dot(low_one, w_key, preferred_element_type=jnp.float32).reshape(
        row_count, KV_HEADS, HD
    )
    value_low = (
        jnp.dot(low_one, w_value, preferred_element_type=jnp.float32)
        .astype(jnp.bfloat16)
        .reshape(row_count, KV_HEADS, HD)
    )
    query_low = (
        rotate(query_pre, cosine, sine_table)
        .astype(jnp.bfloat16)
        .reshape(row_count, KV_HEADS, groups, HD)
    )
    key_low = rotate(key_pre, cosine, sine_table).astype(jnp.bfloat16)
    scores = (
        jnp.einsum("ikgd,jkd->kgij", query_low, key_low, preferred_element_type=jnp.float32)
        * score_scale
    )
    masked = jnp.where(allowed[None, None], scores, MASKED_SCORE)
    row_max = jnp.max(masked, axis=-1, keepdims=True)
    exp_scores = jnp.exp(masked - row_max)
    row_total = jnp.sum(exp_scores, axis=-1, keepdims=True)
    log_total = row_max + jnp.log(row_total)
    prob_rows = (exp_scores / row_total).astype(jnp.bfloat16)
    attended = jnp.einsum(
        "kgij,jkd->ikgd", prob_rows, value_low, preferred_element_type=jnp.float32
    )
    attended_low = attended.reshape(row_count, HEADS * HD).astype(jnp.bfloat16)
    middle = inputs + jnp.dot(attended_low, w_out, preferred_element_type=jnp.float32)
    scale_two = rms_scale(middle)
    normed_two = middle * scale_two
    low_two = (normed_two * feedforward_gain).astype(jnp.bfloat16)
    gate_pre = jnp.dot(low_two, w_gate, preferred_element_type=jnp.float32)
    upward = jnp.dot(low_two, w_up, preferred_element_type=jnp.float32)
    sigmoid_gate = jax.nn.sigmoid(gate_pre)
    silu_gate = gate_pre * sigmoid_gate
    hidden_low = (silu_gate * upward).astype(jnp.bfloat16)
    branch_two = jnp.dot(hidden_low, w_down, preferred_element_type=jnp.float32)
    layer_out = (row_valid[:, None] * (middle + branch_two)).astype(jnp.bfloat16)
    grad_out = row_valid[:, None] * cotangent.astype(jnp.float32)
    grad_out_low = grad_out.astype(jnp.bfloat16)
    grad_wdown = outer_sum(hidden_low, grad_out_low)
    grad_hidden = times_t(grad_out_low, w_down).astype(jnp.bfloat16).astype(jnp.float32)
    grad_up = (grad_hidden * silu_gate).astype(jnp.bfloat16)
    grad_gate = (
        grad_hidden * upward * sigmoid_gate * (1.0 + gate_pre * (1.0 - sigmoid_gate))
    ).astype(jnp.bfloat16)
    grad_wgate = outer_sum(low_two, grad_gate)
    grad_wup = outer_sum(low_two, grad_up)
    grad_norm_two = times_t(grad_gate, w_gate) + times_t(grad_up, w_up)
    grad_gain_two = jnp.sum(grad_norm_two * normed_two, axis=0)
    scaled_two = grad_norm_two * feedforward_gain
    grad_middle = grad_out + scale_two * (
        scaled_two - normed_two * jnp.mean(scaled_two * normed_two, axis=-1, keepdims=True)
    )
    grad_branch_low = grad_middle.astype(jnp.bfloat16)
    grad_wout = outer_sum(attended_low, grad_branch_low)
    grad_attended = (
        times_t(grad_branch_low, w_out)
        .astype(jnp.bfloat16)
        .reshape(row_count, KV_HEADS, groups, HD)
    )
    scores_again = (
        jnp.einsum("ikgd,jkd->kgij", query_low, key_low, preferred_element_type=jnp.float32)
        * score_scale
    )
    probs_again = jnp.exp(jnp.where(allowed[None, None], scores_again, MASKED_SCORE) - log_total)
    grad_value = jnp.einsum(
        "kgij,ikgd->jkd",
        probs_again.astype(jnp.bfloat16),
        grad_attended,
        preferred_element_type=jnp.float32,
    )
    grad_probs = jnp.einsum(
        "ikgd,jkd->kgij", grad_attended, value_low, preferred_element_type=jnp.float32
    )
    inner_sum = jnp.sum(probs_again * grad_probs, axis=-1, keepdims=True)
    grad_scores = (probs_again * (grad_probs - inner_sum)).astype(jnp.bfloat16)
    grad_query = (
        jnp.einsum("kgij,jkd->ikgd", grad_scores, key_low, preferred_element_type=jnp.float32)
        * score_scale
    )
    grad_key = (
        jnp.einsum("kgij,ikgd->jkd", grad_scores, query_low, preferred_element_type=jnp.float32)
        * score_scale
    )
    grad_query_low = (
        unrotate(grad_query.reshape(row_count, HEADS, HD), cosine, sine_table)
        .reshape(row_count, HEADS * HD)
        .astype(jnp.bfloat16)
    )
    grad_key_low = (
        unrotate(grad_key, cosine, sine_table)
        .reshape(row_count, KV_HEADS * HD)
        .astype(jnp.bfloat16)
    )
    grad_value_low = grad_value.reshape(row_count, KV_HEADS * HD).astype(jnp.bfloat16)
    grad_wquery = outer_sum(low_one, grad_query_low)
    grad_wkey = outer_sum(low_one, grad_key_low)
    grad_wvalue = outer_sum(low_one, grad_value_low)
    grad_norm_one = (
        times_t(grad_query_low, w_query)
        + times_t(grad_key_low, w_key)
        + times_t(grad_value_low, w_value)
    )
    grad_gain_one = jnp.sum(grad_norm_one * normed_one, axis=0)
    scaled_one = grad_norm_one * attention_gain
    grad_inputs = grad_middle + scale_one * (
        scaled_one - normed_one * jnp.mean(scaled_one * normed_one, axis=-1, keepdims=True)
    )
    gain_one_sum, gain_two_sum = lax.psum((grad_gain_one, grad_gain_two), "fsdp")
    every_list = (grad_wquery, grad_wkey, grad_wvalue, grad_wout, grad_wgate, grad_wup, grad_wdown)
    every_summed = lax.psum_scatter(
        pack_grads(every_list, count), "fsdp", scatter_dimension=0, tiled=True
    )
    query_shard, key_shard, value_shard, out_shard, gate_shard, up_shard, down_shard = unpack_grads(
        every_summed, every_list, count
    )
    return (
        layer_out,
        grad_inputs.astype(jnp.bfloat16),
        query_shard,
        key_shard,
        value_shard,
        out_shard,
        gate_shard,
        up_shard,
        down_shard,
        gain_one_sum,
        gain_two_sum,
    )


def solution(mesh):
    return jax.shard_map(
        on_device,
        mesh=mesh,
        in_specs=(
            P("fsdp", None),
            P("fsdp", None),
            P(),
            P(),
            P("fsdp"),
            P("fsdp"),
            P("fsdp"),
            P("fsdp"),
            P("fsdp"),
            P("fsdp"),
            P("fsdp"),
            P(),
            P(),
        ),
        out_specs=(
            P("fsdp", None),
            P("fsdp", None),
            P("fsdp"),
            P("fsdp"),
            P("fsdp"),
            P("fsdp"),
            P("fsdp"),
            P("fsdp"),
            P("fsdp"),
            P(),
            P(),
        ),
        check_vma=False,
    )
```

profile of v0, /device:TPU:9, one launch (start us, length us, event | category | flops | bytes accessed | tf_op | source)
XLA Modules:
  0.0 1047.5 jit_solution(9385243289432678324)
XLA Ops:
  26.6 210.8 %all-gather.3.cloned.1.call-done = bf16[32,1,307200]{2,1,0:T(2,128)(2,1)} async-done(((bf16[1,1,307200]{2,1,0:T(2,128)(2,1)}), bf16[32,1,307200]{2,1,0:T(2,128)(2,1)}) %all-gather.3.cloned.1.call-update) | async-done | bytes 19660816 | tf_op jit(solution)/shard_map/all_gather | solution.py:166
  237.4 32.7 %copy.59 = bf16[32,1,307200]{2,0,1:T(8,128)(2,1)S(1)} copy(bf16[32,1,307200]{2,1,0:T(2,128)(2,1)} %all-gather.3.cloned.1.call-done) | data formatting | bytes 39321600
  272.2 5.2 fusion.58
  302.2 10.0 reshape_reshape.25
  312.1 9.7 reshape_reshape.26
  322.1 4.6 fusion.62
  328.6 9.2 reshape_reshape.27
  337.8 6.4 multiply_convert_fusion
  355.7 5.1 fusion.65
  360.8 5.1 fusion.66
  369.3 5.2 reshape.299
  374.5 4.2 constant_dynamic-update-slice_fusion.6
  388.2 5.1 reshape.302
  393.3 10.3 reshape.303
  403.6 10.3 reshape.304
  413.9 6.5 fusion.31
  420.5 10.8 %reshape.305 = f32[32,76800]{1,0:T(8,128)} reshape(f32[2560,960]{1,0:T(8,128)} %fusion.31) | data formatting | bytes 19660800 | tf_op jit(solution)/shard_map/reshape | solution.py:109
  438.4 8.6 constant_dynamic-update-slice_fusion.2
  447.0 4.5 constant_dynamic-update-slice_fusion.1
  451.5 8.1 constant_dynamic-update-slice_fusion
  465.1 42.0 %all-reduce.1 = (f32[960]{0:T(1024)}, f32[960]{0:T(1024)}) all-reduce(f32[960]{0:T(1024)S(1)} %get-tuple-element.17, f32[960]{0:T(1024)S(1)} %copy-done.29), channel_id=1, replica_groups=mesh['fsdp'=32] {'fsdp'}, use_global_device_ids=true, to_apply=%region_13.14 | all-reduce | flops 1920 | bytes 15360 | tf_op jit(solution)/shard_map/psum | solution.py:287
  509.1 5.4 fusion.6
  514.5 515.1 %all-reduce.4.cloned.1.call-done = f32[32,307200]{1,0:T(8,128)} async-done(((f32[32,307200]{1,0:T(8,128)}), f32[32,307200]{1,0:T(8,128)}) %all-reduce.4.cloned.1.call-update) | async-done | bytes 39321616
  1034.4 6.0 fusion.57
  (154 shorter events, 90.2 us)
Async XLA Ops:
  7.2 230.2 %all-gather.3.cloned.1.call-start = ((), (), s32[]{:S(2)}) async-start(), calls=%async_computation | async-start | bytes 40550400 | tf_op jit(solution)/shard_map/all_gather | solution.py:166
  15.0 1014.6 %all-reduce.4.cloned.1.call-start = ((), (), s32[]{:S(2)}) async-start(), calls=%async_computation.1 | async-start | bytes 78643200
  25.2 267.3 %copy-start.27 = (f32[128]{0:T(128)}, f32[128]{0:T(128)S(1)}, u32[]{:S(2)}) copy-start(f32[128]{0:T(128)S(1)} %add_rsqrt_fusion.1) | copy-start | bytes 1540
  279.1 5.5 copy-start.1
  279.1 5.5 copy-start.19
  284.6 8.3 copy-start.15
  284.6 8.3 copy-start.17
  287.0 6.1 copy-start.30
  293.1 6.6 copy-start.21
  293.1 6.6 copy-start.23
  295.7 16.5 %copy-start.11 = (bf16[5,64,3,128]{3,1,2,0:T(8,128)(2,1)}, bf16[5,64,3,128]{3,1,2,0:T(8,128)(2,1)S(1)}, u32[]{:S(2)}) copy-start(bf16[5,64,3,128]{3,1,2,0:T(8,128)(2,1)S(1)} %convolution_convert_fusion.2) | copy-start | bytes 737284
  302.2 19.7 %copy-start.33 = (f32[128]{0:T(128)}, f32[128]{0:T(128)S(1)}, u32[]{:S(2)}) copy-start(f32[128]{0:T(128)S(1)} %add_rsqrt_fusion) | copy-start | bytes 1540
  312.1 9.8 copy-start.26
  322.1 6.5 copy-start.6
  328.6 19.5 %slice-start = ((s8[4915200]{0:T(1024)(128)(4,1)}), s8[720896]{0:T(1024)(128)(4,1)S(1)}, s32[]{:S(2)}) async-start(s8[4915200]{0:T(1024)(128)(4,1)} %bitcast.104), calls=%async_computation.2 | async-start | bytes 1441792
  337.8 10.3 slice-start.1
  360.8 5.1 copy-start.16
  360.8 5.1 copy-start.18
  360.8 6.0 copy-start.28
  403.6 10.3 copy-start.32
  436.3 10.7 %slice-start.2 = ((s8[9830400]{0:T(1024)(128)(4,1)}), s8[4194304]{0:T(1024)(128)(4,1)S(1)}, s32[]{:S(2)}) async-start(s8[9830400]{0:T(1024)(128)(4,1)} %bitcast.106), calls=%async_computation.4 | async-start | bytes 8388608
  438.4 8.6 slice-start.3
  438.4 8.6 slice-start.4
  459.7 5.4 copy-start.29
  (18 other events, 38.6 us)
Sparse Core Ops, SparseCore 0:
  15.1 222.2 all-gather.2
  459.8 569.7 all-reduce.3
where the time goes:
time: 1060 us; the launch traced here: 1050 us
  waiting for transfers between devices  726 us (68%)
  local copies, waits for them, and re-layouts  184 us (17%)
  matrix products  65.9 us (6%)
  blocking collectives  42 us (4%)
  between operations  16.1 us (2%)
  other arithmetic  14 us (1%)
    unnamed x3, waiting for transfers between devices  515 us
    all_gather x1, waiting for transfers between devices, on_device(): lax.all_gather(pack_shards(shard_list), 'fsdp', axis=0, tiled=True)  211 us
    unnamed x93, local copies, waits for them, and re-layouts  64.9 us
    reshape x7, local copies, waits for them, and re-layouts, pack_grads(): item.reshape(count, -1)  48 us
    psum x1, blocking collectives, on_device(): lax.psum((grad_gain_one, grad_gain_two), 'fsdp')  42 us
    dot_general x7, matrix products, outer_sum(): lax.dot_general(left_side, right_side, (((0,), (0,)), ((), ())), preferre...  25 us
  transfers between devices with their start and end apart: 2, of which 2 were waited for; matrix products, arithmetic and copies ran while one was open for 2% of the time, Pallas kernels for 0%

commit v1 on v0

--- a/solution.py
+++ b/solution.py
@@ -307,9 +307,265 @@
     )
 
 
+BLOCK = 32
+
+
+def pad_rows(block, spare):
+    return jnp.pad(block, ((0, spare), (0, 0)))
+
+
+def spread(values, count):
+    rows = values.shape[0]
+    wide = values.reshape(rows, count, -1)
+    return jnp.pad(wide, ((0, 0), (0, 0), (0, BLOCK - wide.shape[2]))).reshape(rows, count * BLOCK)
+
+
+def gather_in(values, count, width):
+    rows = values.shape[0]
+    return values.reshape(rows, count, BLOCK)[:, :, :width].reshape(rows, count * width)
+
+
+def paired_on_device(
+    tokens,
+    cotangent,
+    seq_lengths,
+    seq_owner,
+    query_weight,
+    key_weight,
+    value_weight,
+    out_weight,
+    gate_weight,
+    up_weight,
+    down_weight,
+    attention_gain,
+    feedforward_gain,
+):
+    row_count = tokens.shape[0]
+    groups = HEADS // KV_HEADS
+    score_scale = 1.0 / math.sqrt(HD)
+    count = lax.axis_size("fsdp")
+    chips = count // 2
+    width = D // count
+    units = FF // count
+    spare = BLOCK - width
+    device = lax.axis_index("fsdp")
+    core = device % 2
+    swap = [(i, i ^ 1) for i in range(count)]
+    chip_groups = [[2 * k + side for k in range(chips)] for side in range(2)]
+
+    def other_core(values):
+        return lax.ppermute(values, "fsdp", swap)
+
+    def in_core_order(mine, theirs, axis):
+        return jnp.where(
+            core == 0,
+            jnp.concatenate([mine, theirs], axis=axis),
+            jnp.concatenate([theirs, mine], axis=axis),
+        )
+
+    def take_core(pair, index):
+        return lax.dynamic_index_in_dim(pair, index, axis=0, keepdims=False)
+
+    def gather_chips(block):
+        return lax.all_gather(block, "fsdp", axis_index_groups=chip_groups, axis=0, tiled=False)
+
+    def scatter_chips(blocks):
+        return lax.psum_scatter(
+            blocks,
+            "fsdp",
+            scatter_dimension=0,
+            axis_index_groups=chip_groups,
+            tiled=False,
+        )
+
+    attention_shard = pad_rows(
+        jnp.concatenate(
+            [
+                query_weight.reshape(width, HEADS * HD),
+                key_weight.reshape(width, KV_HEADS * HD),
+                value_weight.reshape(width, KV_HEADS * HD),
+                out_weight.reshape(width, D),
+            ],
+            axis=1,
+        ),
+        spare,
+    )
+    attention_mine = gather_chips(attention_shard)
+    attention_other = other_core(attention_mine)
+
+    gate_up = jnp.stack([gate_weight.reshape(width, chips, 2, units), up_weight.reshape(width, chips, 2, units)])
+    gate_up = gate_up.transpose(3, 0, 1, 2, 4).reshape(2, 2, width, chips * units)
+    gate_up = jnp.pad(gate_up, ((0, 0), (0, 0), (0, spare), (0, 0)))
+    gate_up_other = other_core(take_core(gate_up, 1 - core))
+    gate_up_pair = in_core_order(take_core(gate_up, core), gate_up_other, 1)
+    gate_up_all = gather_chips(gate_up_pair)
+    w_gate = gate_up_all[:, 0].reshape(count * BLOCK, chips * units)
+    w_up = gate_up_all[:, 1].reshape(count * BLOCK, chips * units)
+    w_down = gather_chips(down_weight.reshape(units, D)).reshape(chips * units, D)
+
+    attention_all = in_core_order(attention_mine[:, None], attention_other[:, None], 1).reshape(
+        count * BLOCK, 2 * HEADS * HD + 2 * KV_HEADS * HD
+    )
+    wide_qkv = (HEADS + 2 * KV_HEADS) * HD
+    w_qkv = attention_all[:, :wide_qkv]
+    w_out = attention_all[:, wide_qkv:]
+
+    position, row_valid, allowed = own_rows(seq_lengths, seq_owner, device, row_count)
+    cosine, sine_table = rope_tables(position, HD)
+    grad_out = row_valid[:, None] * cotangent.astype(jnp.float32)
+    grad_out_low = grad_out.astype(jnp.bfloat16)
+    grad_out_both = jnp.concatenate([grad_out_low, other_core(grad_out_low)], axis=0)
+
+    inputs = tokens.astype(jnp.float32)
+    scale_one = rms_scale(inputs)
+    normed_one = inputs * scale_one
+    low_one = spread((normed_one * attention_gain).astype(jnp.bfloat16), count)
+    qkv = jnp.dot(low_one, w_qkv, preferred_element_type=jnp.float32)
+    query_pre = qkv[:, : HEADS * HD].reshape(row_count, HEADS, HD)
+    key_pre = qkv[:, HEADS * HD : (HEADS + KV_HEADS) * HD].reshape(row_count, KV_HEADS, HD)
+    value_low = qkv[:, (HEADS + KV_HEADS) * HD :].astype(jnp.bfloat16).reshape(row_count, KV_HEADS, HD)
+    query_low = (
+        rotate(query_pre, cosine, sine_table)
+        .astype(jnp.bfloat16)
+        .reshape(row_count, KV_HEADS, groups, HD)
+    )
+    key_low = rotate(key_pre, cosine, sine_table).astype(jnp.bfloat16)
+    scores = (
+        jnp.einsum("ikgd,jkd->kgij", query_low, key_low, preferred_element_type=jnp.float32)
+        * score_scale
+    )
+    masked = jnp.where(allowed[None, None], scores, MASKED_SCORE)
+    row_max = jnp.max(masked, axis=-1, keepdims=True)
+    exp_scores = jnp.exp(masked - row_max)
+    row_total = jnp.sum(exp_scores, axis=-1, keepdims=True)
+    probs = exp_scores / row_total
+    prob_rows = probs.astype(jnp.bfloat16)
+    attended = jnp.einsum(
+        "kgij,jkd->ikgd", prob_rows, value_low, preferred_element_type=jnp.float32
+    )
+    attended_low = spread(attended.reshape(row_count, HEADS * HD).astype(jnp.bfloat16), count)
+    middle = inputs + jnp.dot(attended_low, w_out, preferred_element_type=jnp.float32)
+    scale_two = rms_scale(middle)
+    normed_two = middle * scale_two
+    low_two = spread((normed_two * feedforward_gain).astype(jnp.bfloat16), count)
+    low_two_both = jnp.concatenate([low_two, other_core(low_two)], axis=0)
+
+    gate_pre = jnp.dot(low_two_both, w_gate, preferred_element_type=jnp.float32)
+    upward = jnp.dot(low_two_both, w_up, preferred_element_type=jnp.float32)
+    sigmoid_gate = jax.nn.sigmoid(gate_pre)
+    silu_gate = gate_pre * sigmoid_gate
+    hidden_low = (silu_gate * upward).astype(jnp.bfloat16)
+    branch_both = jnp.dot(hidden_low, w_down, preferred_element_type=jnp.float32)
+    branch_two = branch_both[:row_count] + other_core(branch_both[row_count:])
+    layer_out = (row_valid[:, None] * (middle + branch_two)).astype(jnp.bfloat16)
+
+    grad_wdown = outer_sum(hidden_low, grad_out_both).astype(jnp.bfloat16)
+    down_sum = scatter_chips(grad_wdown.reshape(chips, units, D))
+    grad_hidden = times_t(grad_out_both, w_down).astype(jnp.bfloat16).astype(jnp.float32)
+    grad_up = (grad_hidden * silu_gate).astype(jnp.bfloat16)
+    grad_gate = (
+        grad_hidden * upward * sigmoid_gate * (1.0 + gate_pre * (1.0 - sigmoid_gate))
+    ).astype(jnp.bfloat16)
+    grad_wgate = outer_sum(low_two_both, grad_gate).astype(jnp.bfloat16)
+    grad_wup = outer_sum(low_two_both, grad_up).astype(jnp.bfloat16)
+    gate_up_sum = scatter_chips(
+        jnp.concatenate(
+            [
+                grad_wgate.reshape(chips, 2 * BLOCK, chips * units),
+                grad_wup.reshape(chips, 2 * BLOCK, chips * units),
+            ],
+            axis=1,
+        )
+    )
+    grad_norm_both = times_t(grad_gate, w_gate) + times_t(grad_up, w_up)
+    grad_norm_two = gather_in(
+        grad_norm_both[:row_count] + other_core(grad_norm_both[row_count:]), count, width
+    )
+    grad_gain_two = jnp.sum(grad_norm_two * normed_two, axis=0)
+    scaled_two = grad_norm_two * feedforward_gain
+    grad_middle = grad_out + scale_two * (
+        scaled_two - normed_two * jnp.mean(scaled_two * normed_two, axis=-1, keepdims=True)
+    )
+    grad_branch_low = grad_middle.astype(jnp.bfloat16)
+    grad_wout = outer_sum(attended_low, grad_branch_low)
+    grad_attended = gather_in(
+        times_t(grad_branch_low, w_out).astype(jnp.bfloat16), count, width
+    ).reshape(row_count, KV_HEADS, groups, HD)
+    grad_value = jnp.einsum(
+        "kgij,ikgd->jkd", prob_rows, grad_attended, preferred_element_type=jnp.float32
+    )
+    grad_probs = jnp.einsum(
+        "ikgd,jkd->kgij", grad_attended, value_low, preferred_element_type=jnp.float32
+    )
+    inner_sum = jnp.sum(probs * grad_probs, axis=-1, keepdims=True)
+    grad_scores = (probs * (grad_probs - inner_sum)).astype(jnp.bfloat16)
+    grad_query = (
+        jnp.einsum("kgij,jkd->ikgd", grad_scores, key_low, preferred_element_type=jnp.float32)
+        * score_scale
+    )
+    grad_key = (
+        jnp.einsum("kgij,ikgd->jkd", grad_scores, query_low, preferred_element_type=jnp.float32)
+        * score_scale
+    )
+    grad_qkv = jnp.concatenate(
+        [
+            unrotate(grad_query.reshape(row_count, HEADS, HD), cosine, sine_table)
+            .reshape(row_count, HEADS * HD)
+            .astype(jnp.bfloat16),
+            unrotate(grad_key, cosine, sine_table)
+            .reshape(row_count, KV_HEADS * HD)
+            .astype(jnp.bfloat16),
+            grad_value.reshape(row_count, KV_HEADS * HD).astype(jnp.bfloat16),
+        ],
+        axis=1,
+    )
+    grad_wqkv = outer_sum(low_one, grad_qkv)
+    grad_attention = jnp.concatenate([grad_wqkv, grad_wout], axis=1).reshape(
+        chips, 2, BLOCK, 2 * HEADS * HD + 2 * KV_HEADS * HD
+    )
+    keep = lax.dynamic_index_in_dim(grad_attention, core, axis=1, keepdims=False)
+    give = lax.dynamic_index_in_dim(grad_attention, 1 - core, axis=1, keepdims=False)
+    attention_sum = scatter_chips(
+        (keep + other_core(give.astype(jnp.bfloat16)).astype(jnp.float32)).astype(jnp.bfloat16)
+    )[:width].astype(jnp.float32)
+
+    grad_norm_one = gather_in(times_t(grad_qkv, w_qkv), count, width)
+    grad_gain_one = jnp.sum(grad_norm_one * normed_one, axis=0)
+    scaled_one = grad_norm_one * attention_gain
+    grad_inputs = grad_middle + scale_one * (
+        scaled_one - normed_one * jnp.mean(scaled_one * normed_one, axis=-1, keepdims=True)
+    )
+    gain_sums = jnp.sum(
+        lax.all_gather(jnp.stack([grad_gain_one, grad_gain_two]), "fsdp", axis=0), axis=0
+    )
+
+    gate_up_sum = gate_up_sum.reshape(2, 2, BLOCK, chips * units).transpose(1, 0, 2, 3)
+    gate_up_got = other_core(take_core(gate_up_sum, 1 - core))
+    gate_up_kept = take_core(gate_up_sum, core)
+    halves = in_core_order(gate_up_kept[None], gate_up_got[None], 0)[:, :, :width]
+    halves = halves.reshape(2, 2, width, chips, units).transpose(1, 2, 3, 0, 4).astype(jnp.float32)
+    edge_key, edge_value = HEADS * HD, (HEADS + KV_HEADS) * HD
+    return (
+        layer_out,
+        grad_inputs.astype(jnp.bfloat16),
+        attention_sum[:, :edge_key].reshape(-1),
+        attention_sum[:, edge_key:edge_value].reshape(-1),
+        attention_sum[:, edge_value:wide_qkv].reshape(-1),
+        attention_sum[:, wide_qkv:].reshape(-1),
+        halves[0].reshape(-1),
+        halves[1].reshape(-1),
+        down_sum.astype(jnp.float32).reshape(-1),
+        gain_sums[0],
+        gain_sums[1],
+    )
+
+
 def solution(mesh):
+    count = mesh.shape["fsdp"]
+    whole_rows = count % 2 == 0 and D % count == 0 and FF % count == 0 and D // count <= BLOCK
+    program = paired_on_device if whole_rows else on_device
     return jax.shard_map(
-        on_device,
+        program,
         mesh=mesh,
         in_specs=(
             P("fsdp", None),

time: 1060 us -> 542 us (0.51)
  waiting for transfers between devices: 726 us -> 348 us
  local copies, waits for them, and re-layouts: 184 us -> 54.3 us
  matrix products: 65.9 us -> 40.7 us
  other arithmetic: 14 us -> 37.5 us
    unnamed x3 -> x6, waiting for transfers between devices: 515 us -> 0.1 us
    reduce_scatter x0 -> x3, waiting for transfers between devices: none -> 169 us  [scatter_chips(): lax.psum_scatter(blocks, 'fsdp', scatter_dimension=0, axis_index_groups=c...]
    unnamed x93 -> x96, local copies, waits for them, and re-layouts: 64.9 us -> 5.92 us
    psum x1 -> x0, blocking collectives: 42 us -> none  [on_device(): lax.psum((grad_gain_one, grad_gain_two), 'fsdp')]
    reshape x7 -> x13, local copies, waits for them, and re-layouts: 48 us -> 9.18 us  [the longest x2 1.11 us: gather_in(): values.reshape(rows, count, BLOCK)[:, :, :width]]
    all_gather x1 -> x3, waiting for transfers between devices: 211 us -> 174 us  [gather_chips(): lax.all_gather(block, 'fsdp', axis_index_groups=chip_groups, axis=0, tile...]
    all_gather x0 -> x1, blocking collectives: none -> 34.7 us  [paired_on_device(): lax.all_gather(jnp.stack([grad_gain_one, grad_gain_two]), 'fsdp', axis=0)]
    another operation x7, local copies, waits for them, and re-layouts: 39.4 us -> 7.33 us  [the longest x2 2.37 us: paired_on_device(): jnp.stack([gate_weight.reshape(width, chips, 2, units), up_weight.reshape...]
  transfers between devices with their start and end apart: 2 -> 14, of which waited for: 2 -> 7; matrix products, arithmetic and copies ran while one was open for 2% -> 20% of each run, Pallas kernels for 0% -> 0%
where the time goes in v1:
time: 542 us; the launch traced here: 538 us
  waiting for transfers between devices  348 us (64%)
  local copies, waits for them, and re-layouts  54.3 us (10%)
  matrix products  40.7 us (8%)
  other arithmetic  37.5 us (7%)
  blocking collectives  34.7 us (6%)
  between operations  16.4 us (3%)
  starting transfers between devices  6.39 us (1%)
    all_gather x3, waiting for transfers between devices, gather_chips(): lax.all_gather(block, 'fsdp', axis_index_groups=chip_groups, axis=0, tile...  174 us
    reduce_scatter x3, waiting for transfers between devices, scatter_chips(): lax.psum_scatter(blocks, 'fsdp', scatter_dimension=0, axis_index_groups=c...  169 us
    all_gather x1, blocking collectives, paired_on_device(): lax.all_gather(jnp.stack([grad_gain_one, grad_gain_two]), 'fsdp', axis=0)  34.7 us
    dot_general x5, matrix products, outer_sum(): lax.dot_general(left_side, right_side, (((0,), (0,)), ((), ())), preferre...  11.9 us
    dot_general x5, matrix products, times_t(): lax.dot_general(left_side, right_side, (((1,), (1,)), ((), ())), preferre...  11.8 us
    concatenate x1, local copies, waits for them, and re-layouts, paired_on_device(): jnp.concatenate([grad_wqkv, grad_wout], axis=1)  11.6 us
  transfers between devices with their start and end apart: 14, of which 7 were waited for; matrix products, arithmetic and copies ran while one was open for 20% of the time, Pallas kernels for 0%

profile of v1, /device:TPU:9, one launch (start us, length us, event | category | flops | bytes accessed | tf_op | source)
XLA Modules:
  0.0 538.2 jit_solution(8576346550275643792)
XLA Ops:
  19.4 57.3 %all-gather.11.cloned.1.call-done = bf16[512,2560]{1,0:T(8,128)(2,1)} async-done(((bf16[32,2560]{1,0:T(8,128)(2,1)}), bf16[512,2560]{1,0:T(8,128)(2,1)}) %all-gather.11.cloned.1.call-update) | async-done | bytes 2621456 | tf_op jit(solution)/shard_map/all_gather | solution.py:370
  88.8 4.0 maximum_select_fusion
  99.0 3.5 multiply_reduce_fusion.3
  103.9 58.5 %all-gather.7.cloned.1.call-done = bf16[16,2,64,1280]{3,2,1,0:T(8,128)(2,1)} async-done(((bf16[1,2,64,1280]{3,2,1,0:T(8,128)(2,1)}), bf16[16,2,64,1280]{3,2,1,0:T(8,128)(2,1)}) %all-gather.7.cloned.1.call-update) | async-done | bytes 5242896 | tf_op jit(solution)/shard_map/all_gather | solution.py:370
  162.4 2.9 fusion.74
  165.3 3.4 fusion.72
  168.7 3.0 fusion.73
  171.7 57.9 %all-gather.9.cloned.1.call-done = bf16[16,80,960]{2,1,0:T(8,128)(2,1)} async-done(((bf16[1,80,960]{2,1,0:T(8,128)(2,1)}), bf16[16,80,960]{2,1,0:T(8,128)(2,1)}) %all-gather.9.cloned.1.call-update) | async-done | bytes 2457616 | tf_op jit(solution)/shard_map/all_gather | solution.py:370
  229.5 4.2 multiply_convert_fusion
  241.9 3.5 copy.75
  250.8 2.1 multiply_add_fusion
  252.9 2.8 fusion.20
  258.9 2.6 fusion.49
  261.6 3.7 fusion.46
  265.3 10.4 %pad_maximum_fusion = f32[1024,2560]{0,1:T(8,128)} fusion(f32[1024,960]{0,1:T(8,128)} %fusion.49, f32[1024,1600]{0,1:T(8,128)} %fusion.46), kind=kLoop, calls=%fused_computation.1 | loop fusion | flops 2621440 | bytes 20971520 | tf_op jit(solution)/shard_map/concatenate | solution.py:523
  275.7 11.6 %copy.70 = f32[1024,2560]{1,0:T(8,128)} copy(f32[1024,2560]{0,1:T(8,128)} %pad_maximum_fusion) | data formatting | bytes 20971520 | tf_op jit(solution)/shard_map/concatenate | solution.py:523
  287.3 2.9 fusion.6
  290.6 4.5 collective-permute-done.6
  295.2 5.0 fusion.1
  305.0 2.7 pad_maximum_fusion.1
  308.7 3.1 fusion.2
  312.3 34.7 %all-gather.2 = f32[32,2,960]{2,1,0:T(2,128)S(1)} all-gather(f32[1,2,960]{2,1,0:T(2,128)S(1)} %maximum_bitcast_fusion.8), channel_id=3, replica_groups=mesh['fsdp'=32] {'fsdp'}, dimensions={0}, use_global_device_ids=true | all-gather | bytes 253440 | tf_op jit(solution)/shard_map/all_gather | solution.py:539
  350.4 41.7 %reduce-scatter.4.cloned.1.call-done = bf16[1,32,2560]{2,1,0:T(8,128)(2,1)} async-done(((bf16[16,32,2560]{2,1,0:T(8,128)(2,1)}), bf16[1,32,2560]{2,1,0:T(8,128)(2,1)}) %reduce-scatter.4.cloned.1.call-update) | async-done | bytes 163856 | tf_op jit(solution)/shard_map/reduce_scatter | solution.py:373
  393.9 127.3 %reduce-scatter.6.cloned.1.call-done = bf16[1,128,1280]{2,1,0:T(8,128)(2,1)} async-done(((bf16[16,128,1280]{2,1,0:T(8,128)(2,1)}), bf16[1,128,1280]{2,1,0:T(8,128)(2,1)}) %reduce-scatter.6.cloned.1.call-update) | async-done | bytes 327696 | tf_op jit(solution)/shard_map/reduce_scatter | solution.py:373
  (214 shorter events, 68.8 us)
Async XLA Ops:
  7.2 69.6 %all-gather.11.cloned.1.call-start = ((), (), s32[]{:S(2)}) async-start(), calls=%async_computation.8 | async-start | bytes 2785280 | tf_op jit(solution)/shard_map/all_gather | solution.py:370
  11.6 150.8 %all-gather.7.cloned.1.call-start = ((), (), s32[]{:S(2)}) async-start(), calls=%async_computation.3 | async-start | bytes 5570560 | tf_op jit(solution)/shard_map/all_gather | solution.py:370
  14.0 64.1 %copy-start.46 = (s32[64]{0:T(128)S(1)}, s32[64]{0:T(128)}, u32[]{:S(2)}) copy-start(s32[64]{0:T(128)} %param.16) | copy-start | bytes 772
  14.1 66.0 %copy-start.45 = (s32[64]{0:T(128)S(1)}, s32[64]{0:T(128)}, u32[]{:S(2)}) copy-start(s32[64]{0:T(128)} %param.15) | copy-start | bytes 772
  14.1 69.8 %copy-start.16 = (bf16[128,960]{0,1:T(8,128)(2,1)S(1)}, bf16[128,960]{0,1:T(8,128)(2,1)}, u32[]{:S(2)}) copy-start(bf16[128,960]{0,1:T(8,128)(2,1)} %param.14) | copy-start | bytes 737284
  14.1 70.8 %copy-start.26 = (bf16[76800]{0:T(1024)(128)(2,1)S(1)}, bf16[76800]{0:T(1024)(128)(2,1)}, u32[]{:S(2)}) copy-start(bf16[76800]{0:T(1024)(128)(2,1)} %param.23) | copy-start | bytes 460804
  14.9 71.5 %copy-start.3 = (bf16[128,960]{0,1:T(8,128)(2,1)S(1)}, bf16[128,960]{0,1:T(8,128)(2,1)}, u32[]{:S(2)}) copy-start(bf16[128,960]{0,1:T(8,128)(2,1)} %param.13) | copy-start | bytes 737284
  14.9 71.6 %copy-start.33 = (f32[960]{0:T(1024)S(1)}, f32[960]{0:T(1024)}, u32[]{:S(2)}) copy-start(f32[960]{0:T(1024)} %param.24) | copy-start | bytes 11524
  16.1 1.8 collective-permute-start.2
  19.4 210.1 %all-gather.9.cloned.1.call-start = ((), (), s32[]{:S(2)}) async-start(), calls=%async_computation.4 | async-start | bytes 2785280 | tf_op jit(solution)/shard_map/all_gather | solution.py:370
  76.7 12.1 %copy-start.9 = (bf16[512,2560]{1,0:T(8,128)(2,1)S(1)}, bf16[512,2560]{1,0:T(8,128)(2,1)}, u32[]{:S(2)}) copy-start(bf16[512,2560]{1,0:T(8,128)(2,1)} %all-gather.11.cloned.1.call-done) | copy-start | bytes 7864324
  76.7 12.1 %collective-permute-start = (bf16[16,32,2560]{2,1,0:T(8,128)(2,1)}, bf16[16,32,2560]{2,1,0:T(8,128)(2,1)}, u32[]{:S(2)}, u32[]{:S(2)}) collective-permute-start(bf16[16,32,2560]{2,1,0:T(8,128)(2,1)} %bitcast.186), channel_id=1, source_target_pairs={{0,1},{1,0},{2,3},{3,2},{4,5},{5,4},{6,7},{7,6},{8,9},{9,8},{10,11... | collective-permute-start | bytes 7864328 | tf_op jit(solution)/shard_map/ppermute | solution.py:357
  84.7 87.0 %collective-permute-start.4 = (bf16[128,960]{0,1:T(8,128)(2,1)}, bf16[128,960]{0,1:T(8,128)(2,1)}, u32[]{:S(2)}, u32[]{:S(2)}) collective-permute-start(bf16[128,960]{0,1:T(8,128)(2,1)} %fusion.42), channel_id=1, source_target_pairs={{0,1},{1,0},{2,3},{3,2},{4,5},{5,4},{6,7},{7,6},{8,9},{9,8},{10,11... | collective-permute-start | bytes 737288 | tf_op jit(solution)/shard_map/ppermute | solution.py:357
  85.7 262.9 %reduce-scatter.8.cloned.1.call-start = ((), (), s32[]{:S(2)}) async-start(), calls=%async_computation.7 | async-start | bytes 2785280 | tf_op jit(solution)/shard_map/reduce_scatter | solution.py:373
  86.6 6.3 %copy-start.39 = (f32[128]{0:T(128)}, f32[128]{0:T(128)S(1)}, u32[]{:S(2)}) copy-start(f32[128]{0:T(128)S(1)} %add_rsqrt_fusion.1) | copy-start | bytes 1540
  88.7 8.2 %copy-start.36 = (pred[128,128]{0,1:T(8,128)(4,1)}, pred[128,128]{0,1:T(8,128)(4,1)S(1)}, u32[]{:S(2)}) copy-start(pred[128,128]{0,1:T(8,128)(4,1)S(1)} %fusion.52) | copy-start | bytes 49156
  103.6 61.7 %collective-permute-start.1 = (bf16[128,1024]{0,1:T(8,128)(2,1)}, bf16[128,1024]{0,1:T(8,128)(2,1)}, u32[]{:S(2)}, u32[]{:S(2)}) collective-permute-start(bf16[128,1024]{0,1:T(8,128)(2,1)} %bitcast.17), channel_id=1, source_target_pairs={{0,1},{1,0},{2,3},{3,2},{4,5},{5,4},{6,7},{7,6},{8,9},{9,8},{10,11... | collective-permute-start | bytes 786440 | tf_op jit(solution)/shard_map/ppermute | solution.py:357
  165.3 6.4 %copy-start.6 = (bf16[16,1,64,1280]{3,2,1,0:T(8,128)(2,1)}, bf16[16,1,64,1280]{3,2,1,0:T(8,128)(2,1)S(1)}, u32[]{:S(2)}) copy-start(bf16[16,1,64,1280]{3,2,1,0:T(8,128)(2,1)S(1)} %get-tuple-element.17) | copy-start | bytes 7864324
  236.4 9.4 %collective-permute-start.5 = (f32[128,1024]{1,0:T(8,128)}, f32[128,1024]{1,0:T(8,128)}, u32[]{:S(2)}, u32[]{:S(2)}) collective-permute-start(f32[128,1024]{1,0:T(8,128)} %slice.144), channel_id=1, source_target_pairs={{0,1},{1,0},{2,3},{3,2},{4,5},{5,4},{6,7},{7,6},{8,9},{9,8},{10,11... | collective-permute-start | bytes 1572872 | tf_op jit(solution)/shard_map/ppermute | solution.py:357
  240.0 10.8 %collective-permute-start.3 = (f32[128,960]{0,1:T(8,128)}, f32[128,960]{0,1:T(8,128)}, u32[]{:S(2)}, u32[]{:S(2)}) collective-permute-start(f32[128,960]{0,1:T(8,128)} %slice.142), channel_id=1, source_target_pairs={{0,1},{1,0},{2,3},{3,2},{4,5},{5,4},{6,7},{7,6},{8,9},{9,8},{10,11... | collective-permute-start | bytes 1474568 | tf_op jit(solution)/shard_map/ppermute | solution.py:357
  245.5 146.6 %reduce-scatter.4.cloned.1.call-start = ((), (), s32[]{:S(2)}) async-start(), calls=%async_computation.5 | async-start | bytes 2785280 | tf_op jit(solution)/shard_map/reduce_scatter | solution.py:373
  290.1 5.0 collective-permute-start.6
  300.2 220.9 %reduce-scatter.6.cloned.1.call-start = ((), (), s32[]{:S(2)}) async-start(), calls=%async_computation.6 | async-start | bytes 5570560 | tf_op jit(solution)/shard_map/reduce_scatter | solution.py:373
  522.3 3.9 collective-permute-start.7
  (37 other events, 98.0 us)
Sparse Core Ops, SparseCore 0:
  11.7 64.9 all-gather.10
  79.5 82.8 all-gather.6
  165.7 63.8 all-gather.8
  245.6 64.5 reduce-scatter.7
  312.3 79.6 reduce-scatter.3
  394.2 126.8 reduce-scatter.5

commit v2 on v1

--- a/solution.py
+++ b/solution.py
@@ -3,6 +3,8 @@
 import jax
 import jax.numpy as jnp
 from jax import lax
+from jax.experimental import pallas as pl
+from jax.experimental.pallas import tpu as pltpu
 from jax.sharding import PartitionSpec as P
 
 D = 960
@@ -308,6 +310,354 @@
 
 
 BLOCK = 32
+LINE = 4
+CHIPS = 16
+MESH = pl.DeviceIdType.MESH
+
+
+def chip_place():
+    device = lax.axis_index("fsdp")
+    core, chip = device % 2, device // 2
+    return core, chip // 4, (chip // 2) % 2, chip % 2
+
+
+def chip_number(z, y, x):
+    return (z * 2 + y) * 2 + x
+
+
+def greet_neighbours(core, z, y, x):
+    barrier = pltpu.get_barrier_semaphore()
+
+    def greet(z_to, y_to, x_to):
+        pl.semaphore_signal(
+            barrier,
+            inc=1,
+            device_id=(chip_number(z_to, y_to, x_to) * 2 + core,),
+            device_id_type=MESH,
+        )
+
+    greet(z, 1 - y, x)
+    greet(z, y, 1 - x)
+
+    @pl.when(z > 0)
+    def _():
+        greet(z - 1, y, x)
+
+    @pl.when(z < LINE - 1)
+    def _():
+        greet(z + 1, y, x)
+
+    pl.semaphore_wait(barrier, jnp.where((z > 0) & (z < LINE - 1), 4, 3))
+
+
+def half_rows(refs, half):
+    result = []
+    for ref in refs:
+        rows = ref.shape[-2]
+        first = (rows // 2 + 15) // 16 * 16
+        result.append(pl.ds(0, first) if half == 0 else pl.ds(first, rows - first))
+    return result
+
+
+def steps_at(distance):
+    return (0,) if distance == 0 else (-distance, distance)
+
+
+def gather_kernel(*refs):
+    ins, outs = refs[0:3], refs[3:6]
+    own_sem, recv_sem, up_sem, down_sem, first_sem, second_sem = refs[6:]
+    core, z, y, x = chip_place()
+    greet_neighbours(core, z, y, x)
+    me = chip_number(z, y, x)
+    rows = [half_rows(ins, half) for half in range(2)]
+    pending = []
+
+    def send(half, source, is_own, sem, slot, target):
+        for i in range(3):
+            span = rows[half][i]
+            src = ins[i].at[span] if is_own else outs[i].at[source, span]
+            copy = pltpu.make_async_remote_copy(
+                src_ref=src,
+                dst_ref=outs[i].at[source, span],
+                send_sem=sem.at[half, i, slot],
+                recv_sem=recv_sem.at[half, i, source],
+                device_id=(target * 2 + core,),
+                device_id_type=MESH,
+            )
+            copy.start()
+            yield copy
+
+    def send_all(condition, *args):
+        def run():
+            for _ in send(*args):
+                pass
+
+        if condition is None:
+            run()
+        else:
+            pl.when(condition)(run)
+        pending.append((condition, args))
+
+    def receive(half, source):
+        for i in range(3):
+            view = outs[i].at[source, rows[half][i]]
+            pltpu.make_async_remote_copy(
+                src_ref=view,
+                dst_ref=view,
+                send_sem=own_sem.at[i],
+                recv_sem=recv_sem.at[half, i, source],
+                device_id=(me * 2 + core,),
+                device_id_type=MESH,
+            ).wait_recv()
+
+    def across(half, place):
+        return (1 - y, x) if (half == 0) == (place == 0) else (y, 1 - x)
+
+    def inside(step):
+        return (z + step >= 0) & (z + step < LINE)
+
+    def spread_line(half, step):
+        z_from = z + step
+        source = chip_number(z_from, y, x)
+        own = step == 0
+        ok = None if own else inside(step)
+        if step >= 0:
+            cond = z > 0 if own else (ok & (z > 0))
+            send_all(cond, half, source, own, down_sem, z_from, chip_number(z - 1, y, x))
+        if step <= 0:
+            cond = z < LINE - 1 if own else (ok & (z < LINE - 1))
+            send_all(cond, half, source, own, up_sem, z_from, chip_number(z + 1, y, x))
+        send_all(ok, half, source, own, first_sem, z_from, chip_number(z, *across(half, 0)))
+        send_all(ok, half, source, own, second_sem, z_from, chip_number(z, *across(half, 1)))
+
+    def spread_side(half, step):
+        z_from = z + step
+        source = chip_number(z_from, *across(half, 0))
+        ok = None if step == 0 else inside(step)
+        if ok is None:
+            receive(half, source)
+        else:
+            pl.when(ok)(lambda: receive(half, source))
+        send_all(
+            ok, half, source, False, second_sem, LINE + z_from, chip_number(z, *across(half, 1))
+        )
+
+    local = [pltpu.make_async_copy(ins[i], outs[i].at[me], own_sem.at[i]) for i in range(3)]
+    for half in range(2):
+        spread_line(half, 0)
+    for copy in local:
+        copy.start()
+    for distance in range(LINE):
+        if distance > 0:
+            for half in range(2):
+                for step in steps_at(distance):
+                    pl.when(inside(step))(
+                        lambda: receive(half, chip_number(z + step, y, x))
+                    )
+                    spread_line(half, step)
+        for half in range(2):
+            for step in steps_at(distance):
+                spread_side(half, step)
+    for half in range(2):
+        y_far, x_far = across(half, 1)
+        for z_from in range(LINE):
+            receive(half, chip_number(z_from, y_far, x_far))
+            receive(half, chip_number(z_from, 1 - y, 1 - x))
+    for copy in local:
+        copy.wait()
+    for condition, (half, source, is_own, sem, slot, target) in pending:
+
+        def finish():
+            for i in range(3):
+                span = rows[half][i]
+                src = ins[i].at[span] if is_own else outs[i].at[source, span]
+                pltpu.make_async_remote_copy(
+                    src_ref=src,
+                    dst_ref=outs[i].at[source, span],
+                    send_sem=sem.at[half, i, slot],
+                    recv_sem=recv_sem.at[half, i, source],
+                    device_id=(target * 2 + core,),
+                    device_id_type=MESH,
+                ).wait_send()
+
+        if condition is None:
+            finish()
+        else:
+            pl.when(condition)(finish)
+
+
+def gather_chips(blocks):
+    dma = pltpu.SemaphoreType.DMA
+    return pl.pallas_call(
+        gather_kernel,
+        out_shape=[jax.ShapeDtypeStruct((CHIPS,) + item.shape, item.dtype) for item in blocks],
+        in_specs=[pl.BlockSpec(memory_space=pl.ANY)] * 3,
+        out_specs=[pl.BlockSpec(memory_space=pl.ANY)] * 3,
+        scratch_shapes=[
+            dma((3,)),
+            dma((2, 3, CHIPS)),
+            dma((2, 3, LINE)),
+            dma((2, 3, LINE)),
+            dma((2, 3, LINE)),
+            dma((2, 3, 2 * LINE)),
+        ],
+        compiler_params=pltpu.CompilerParams(collective_id=1, has_side_effects=True),
+        name="gather_chips",
+    )(*blocks)
+
+
+def scatter_kernel(*refs):
+    ins, outs = refs[0:3], refs[3:6]
+    far, side, low, high = refs[6:9], refs[9:12], refs[12:15], refs[15:18]
+    far_send, far_recv, side_send, side_recv, up_send, low_recv, down_send, high_recv = refs[18:]
+    core, z, y, x = chip_place()
+    greet_neighbours(core, z, y, x)
+    rows = [half_rows(outs, half) for half in range(2)]
+    pending = []
+
+    def across(half, place):
+        return (1 - y, x) if (half == 0) == (place == 0) else (y, 1 - x)
+
+    def inside(step):
+        return (z + step >= 0) & (z + step < LINE)
+
+    def copies(half, source, source_at, buffer, slot, send_sem, recv_sem, target):
+        return [
+            pltpu.make_async_remote_copy(
+                src_ref=source[i].at[source_at, rows[half][i]],
+                dst_ref=buffer[i].at[slot, rows[half][i]],
+                send_sem=send_sem.at[half, i, slot],
+                recv_sem=recv_sem.at[half, i, slot],
+                device_id=(target * 2 + core,),
+                device_id_type=MESH,
+            )
+            for i in range(3)
+        ]
+
+    def send(condition, *args):
+        def run():
+            for copy in copies(*args):
+                copy.start()
+
+        pl.when(condition)(run)
+        pending.append((condition, args))
+
+    def receive(half, buffer, slot, send_sem, recv_sem):
+        for copy in copies(half, buffer, slot, buffer, slot, send_sem, recv_sem, 0):
+            copy.wait_recv()
+
+    def add(half, result, result_at, *terms):
+        for i in range(3):
+            span = rows[half][i]
+            total = None
+            for buffer, slot in terms:
+                value = buffer[i][slot, span, :].astype(jnp.float32)
+                total = value if total is None else total + value
+            if result_at is None:
+                result[i][span, :] = total.astype(jnp.bfloat16)
+            else:
+                result[i][result_at, span, :] = total.astype(jnp.bfloat16)
+
+    def over_side(half, step):
+        z_to = z + step
+        place = across(half, 0)
+
+        def work():
+            receive(half, far, LINE + z_to, far_send, far_recv)
+            add(half, far, LINE + z_to, (far, LINE + z_to), (ins, chip_number(z_to, *place)))
+
+        pl.when(inside(step))(work)
+        send(
+            inside(step), half, far, LINE + z_to, side, z_to, side_send, side_recv, chip_number(z, *place)
+        )
+
+    def over_line(half, step):
+        z_to = z + step
+
+        def work():
+            receive(half, far, z_to, far_send, far_recv)
+            receive(half, side, z_to, side_send, side_recv)
+            add(
+                half, side, z_to, (side, z_to), (far, z_to), (ins, chip_number(z_to, y, x))
+            )
+            if step >= 0:
+
+                @pl.when(z > 0)
+                def _():
+                    receive(half, low, z_to, up_send, low_recv)
+                    add(half, side, z_to, (side, z_to), (low, z_to))
+
+            if step <= 0:
+
+                @pl.when(z < LINE - 1)
+                def _():
+                    receive(half, high, z_to, down_send, high_recv)
+                    add(half, side, z_to, (side, z_to), (high, z_to))
+
+            if step == 0:
+                add(half, outs, None, (side, z_to))
+
+        pl.when(inside(step))(work)
+        if step > 0:
+            send(
+                inside(step), half, side, z_to, low, z_to, up_send, low_recv, chip_number(z + 1, y, x)
+            )
+        if step < 0:
+            send(
+                inside(step), half, side, z_to, high, z_to, down_send, high_recv, chip_number(z - 1, y, x)
+            )
+
+    for distance in reversed(range(LINE)):
+        for step in steps_at(distance):
+            for half in range(2):
+                y_to, x_to = across(half, 1)
+                target = chip_number(z, y_to, x_to)
+                z_to = z + step
+                first = chip_number(z_to, 1 - y, 1 - x)
+                own = chip_number(z_to, y_to, x_to)
+                ok = inside(step)
+                send(ok, half, ins, first, far, LINE + z_to, far_send, far_recv, target)
+                send(ok, half, ins, own, far, z_to, far_send, far_recv, target)
+    for distance in (3, 2, 1, 0, -1):
+        if distance >= 0:
+            for step in steps_at(distance):
+                for half in range(2):
+                    over_side(half, step)
+        if distance < LINE - 1:
+            for step in steps_at(distance + 1):
+                for half in range(2):
+                    over_line(half, step)
+    for condition, args in pending:
+
+        def finish():
+            for copy in copies(*args):
+                copy.wait_send()
+
+        pl.when(condition)(finish)
+
+
+def scatter_chips(blocks):
+    dma = pltpu.SemaphoreType.DMA
+
+    def slots(number):
+        return [pltpu.VMEM((number,) + item.shape[1:], item.dtype) for item in blocks]
+
+    return pl.pallas_call(
+        scatter_kernel,
+        out_shape=[jax.ShapeDtypeStruct(item.shape[1:], item.dtype) for item in blocks],
+        in_specs=[pl.BlockSpec(memory_space=pltpu.VMEM)] * 3,
+        out_specs=[pl.BlockSpec(memory_space=pltpu.VMEM)] * 3,
+        scratch_shapes=slots(2 * LINE)
+        + slots(LINE)
+        + slots(LINE)
+        + slots(LINE)
+        + [dma((2, 3, 2 * LINE))] * 2
+        + [dma((2, 3, LINE))] * 6,
+        compiler_params=pltpu.CompilerParams(
+            collective_id=2, has_side_effects=True, vmem_limit_bytes=44 * 1024 * 1024
+        ),
+        name="scatter_chips",
+    )(*blocks)
 
 
 def pad_rows(block, spare):
@@ -351,7 +701,6 @@
     device = lax.axis_index("fsdp")
     core = device % 2
     swap = [(i, i ^ 1) for i in range(count)]
-    chip_groups = [[2 * k + side for k in range(chips)] for side in range(2)]
 
     def other_core(values):
         return lax.ppermute(values, "fsdp", swap)
@@ -365,18 +714,6 @@
 
     def take_core(pair, index):
         return lax.dynamic_index_in_dim(pair, index, axis=0, keepdims=False)
-
-    def gather_chips(block):
-        return lax.all_gather(block, "fsdp", axis_index_groups=chip_groups, axis=0, tiled=False)
-
-    def scatter_chips(blocks):
-        return lax.psum_scatter(
-            blocks,
-            "fsdp",
-            scatter_dimension=0,
-            axis_index_groups=chip_groups,
-            tiled=False,
-        )
 
     attention_shard = pad_rows(
         jnp.concatenate(
@@ -390,18 +727,22 @@
         ),
         spare,
     )
-    attention_mine = gather_chips(attention_shard)
-    attention_other = other_core(attention_mine)
-
     gate_up = jnp.stack([gate_weight.reshape(width, chips, 2, units), up_weight.reshape(width, chips, 2, units)])
     gate_up = gate_up.transpose(3, 0, 1, 2, 4).reshape(2, 2, width, chips * units)
     gate_up = jnp.pad(gate_up, ((0, 0), (0, 0), (0, spare), (0, 0)))
     gate_up_other = other_core(take_core(gate_up, 1 - core))
     gate_up_pair = in_core_order(take_core(gate_up, core), gate_up_other, 1)
-    gate_up_all = gather_chips(gate_up_pair)
-    w_gate = gate_up_all[:, 0].reshape(count * BLOCK, chips * units)
-    w_up = gate_up_all[:, 1].reshape(count * BLOCK, chips * units)
-    w_down = gather_chips(down_weight.reshape(units, D)).reshape(chips * units, D)
+    attention_mine, gate_up_all, down_all = gather_chips(
+        [
+            attention_shard,
+            gate_up_pair.reshape(4 * BLOCK, chips * units),
+            down_weight.reshape(units, D),
+        ]
+    )
+    attention_other = other_core(attention_mine)
+    w_gate = gate_up_all[:, : 2 * BLOCK].reshape(count * BLOCK, chips * units)
+    w_up = gate_up_all[:, 2 * BLOCK :].reshape(count * BLOCK, chips * units)
+    w_down = down_all.reshape(chips * units, D)
 
     attention_all = in_core_order(attention_mine[:, None], attention_other[:, None], 1).reshape(
         count * BLOCK, 2 * HEADS * HD + 2 * KV_HEADS * HD
@@ -460,7 +801,6 @@
     layer_out = (row_valid[:, None] * (middle + branch_two)).astype(jnp.bfloat16)
 
     grad_wdown = outer_sum(hidden_low, grad_out_both).astype(jnp.bfloat16)
-    down_sum = scatter_chips(grad_wdown.reshape(chips, units, D))
     grad_hidden = times_t(grad_out_both, w_down).astype(jnp.bfloat16).astype(jnp.float32)
     grad_up = (grad_hidden * silu_gate).astype(jnp.bfloat16)
     grad_gate = (
@@ -468,14 +808,12 @@
     ).astype(jnp.bfloat16)
     grad_wgate = outer_sum(low_two_both, grad_gate).astype(jnp.bfloat16)
     grad_wup = outer_sum(low_two_both, grad_up).astype(jnp.bfloat16)
-    gate_up_sum = scatter_chips(
-        jnp.concatenate(
-            [
-                grad_wgate.reshape(chips, 2 * BLOCK, chips * units),
-                grad_wup.reshape(chips, 2 * BLOCK, chips * units),
-            ],
-            axis=1,
-        )
+    grad_gate_up = jnp.concatenate(
+        [
+            grad_wgate.reshape(chips, 2 * BLOCK, chips * units),
+            grad_wup.reshape(chips, 2 * BLOCK, chips * units),
+        ],
+        axis=1,
     )
     grad_norm_both = times_t(grad_gate, w_gate) + times_t(grad_up, w_up)
     grad_norm_two = gather_in(
@@ -525,9 +863,14 @@
     )
     keep = lax.dynamic_index_in_dim(grad_attention, core, axis=1, keepdims=False)
     give = lax.dynamic_index_in_dim(grad_attention, 1 - core, axis=1, keepdims=False)
-    attention_sum = scatter_chips(
-        (keep + other_core(give.astype(jnp.bfloat16)).astype(jnp.float32)).astype(jnp.bfloat16)
-    )[:width].astype(jnp.float32)
+    attention_sum, gate_up_sum, down_sum = scatter_chips(
+        [
+            (keep + other_core(give.astype(jnp.bfloat16)).astype(jnp.float32)).astype(jnp.bfloat16),
+            grad_gate_up,
+            grad_wdown.reshape(chips, units, D),
+        ]
+    )
+    attention_sum = attention_sum[:width].astype(jnp.float32)
 
     grad_norm_one = gather_in(times_t(grad_qkv, w_qkv), count, width)
     grad_gain_one = jnp.sum(grad_norm_one * normed_one, axis=0)
@@ -562,7 +905,7 @@
 
 def solution(mesh):
     count = mesh.shape["fsdp"]
-    whole_rows = count % 2 == 0 and D % count == 0 and FF % count == 0 and D // count <= BLOCK
+    whole_rows = count == 2 * CHIPS
     program = paired_on_device if whole_rows else on_device
     return jax.shard_map(
         program,

time: 542 us -> 380 us (0.70)
  waiting for transfers between devices: 348 us -> 0.55 us
  Pallas kernels: 0 us -> 208 us
  between operations: 16.4 us -> 3.52 us
  local copies, waits for them, and re-layouts: 54.3 us -> 47 us
  matrix products: 40.7 us -> 34.4 us
    pallas_call x0 -> x2, Pallas kernels: none -> 208 us  [the longest x1 116 us: scatter_chips(): pl.pallas_call(scatter_kernel, out_shape=[jax.ShapeDtypeStruct(item.shape...]
    all_gather x3 -> x0, waiting for transfers between devices: 174 us -> none  [gather_chips(): lax.all_gather(block, 'fsdp', axis_index_groups=chip_groups, axis=0, tile...]
    reduce_scatter x3 -> x0, waiting for transfers between devices: 169 us -> none  [scatter_chips(): lax.psum_scatter(blocks, 'fsdp', scatter_dimension=0, axis_index_groups=c...]
  transfers between devices with their start and end apart: 14 -> 8, of which waited for: 7 -> 1; matrix products, arithmetic and copies ran while one was open for 20% -> 15% of each run, Pallas kernels for 0% -> 0%
where the time goes in v2:
time: 380 us; the launch traced here: 375 us
  Pallas kernels  208 us (55%)
  local copies, waits for them, and re-layouts  47 us (12%)
  other arithmetic  37.8 us (10%)
  blocking collectives  36.7 us (10%)
  matrix products  34.4 us (9%)
  starting transfers between devices  6.42 us (2%)
    pallas_call x1, Pallas kernels, scatter_chips(): pl.pallas_call(scatter_kernel, out_shape=[jax.ShapeDtypeStruct(item.shape...  116 us
    pallas_call x1, Pallas kernels, gather_chips(): pl.pallas_call(gather_kernel, out_shape=[jax.ShapeDtypeStruct((CHIPS,) +...  92.3 us
    all_gather x1, blocking collectives, paired_on_device(): lax.all_gather(jnp.stack([grad_gain_one, grad_gain_two]), 'fsdp', axis=0)  36.7 us
    dot_general x5, matrix products, outer_sum(): lax.dot_general(left_side, right_side, (((0,), (0,)), ((), ())), preferre...  12.9 us
    concatenate x1, local copies, waits for them, and re-layouts, paired_on_device(): jnp.concatenate([grad_wqkv, grad_wout], axis=1)  11.5 us
    concatenate x1, other arithmetic, paired_on_device(): jnp.concatenate([grad_wqkv, grad_wout], axis=1)  10.1 us
    dot_general x5, matrix products, times_t(): lax.dot_general(left_side, right_side, (((1,), (1,)), ((), ())), preferre...  9.11 us
  transfers between devices with their start and end apart: 8, of which 1 were waited for; matrix products, arithmetic and copies ran while one was open for 15% of the time, Pallas kernels for 0%

profile of v2, /device:TPU:9, one launch (start us, length us, event | category | flops | bytes accessed | tf_op | source)
XLA Modules:
  0.0 374.7 jit_solution(14746734218776319667)
XLA Ops:
  8.9 92.3 %gather_chips.1 = (bf16[16,32,2560]{2,1,0:T(8,128)(2,1)}, bf16[16,128,1280]{2,1,0:T(8,128)(2,1)}, bf16[16,80,960]{2,1,0:T(8,128)(2,1)}) custom-call(bf16[32,2560]{1,0:T(8,128)(2,1)} %pad.19.refs_0_, bf16[128,1280]{1,0:T(8,128)(2,1)} %bitcast.199, bf16[80,960]{1,0:T(8,128)(2,1)} %reshape.317.refs_2_), custom_call_target="tpu_custom_call" | custom-call | tf_op jit(solution)/shard_map/gather_chips/pallas_call | solution.py:491
  101.2 1.9 collective-permute-start.1
  105.0 1.9 fusion.55
  112.8 4.3 %maximum_select_fusion = bf16[16,2,32,2560]{3,2,0,1:T(8,128)(2,1)S(1)} fusion(bf16[16,1,32,2560]{3,2,0,1:T(8,128)(2,1)S(1)} %bitcast.188, bf16[16,1,32,2560]{3,2,0,1:T(8,128)(2,1)} %bitcast.187, pred[]{:T(512)S(6)} %eq.68), kind=kLoop, calls=%fused_computation.2 | loop fusion | flops 7864320 | bytes 10485761 | tf_op jit(solution)/shard_map/jit(_where)/select_n | solution.py:709
  123.0 3.6 multiply_reduce_fusion.3
  128.1 2.9 fusion.72
  133.6 2.5 multiply_convert_fusion
  142.3 2.1 multiply_add_fusion
  144.4 3.0 fusion.20
  150.7 2.7 fusion.47
  154.2 3.8 %fusion.46 = f32[1024,1600]{0,1:T(8,128)} fusion(bf16[128,1024]{0,1:T(8,128)(2,1)S(1)} %bitcast.198, bf16[128,320]{0,1:T(8,128)(2,1)S(1)} %bitcast.222, bf16[128,320]{0,1:T(8,128)(2,1)S(1)} %bitcast.217, bf16[128,960]{0,1:T(8,128)(2,1)S(1)} %bitcast.203), kind=kOutput, calls=%fused_computation.91 | convolution fusion | flops 420659200 | bytes 7225344 | tf_op jit(solution)/shard_map/dot_general | solution.py:85
  158.0 10.1 %pad_maximum_fusion = f32[1024,2560]{0,1:T(8,128)} fusion(f32[1024,960]{0,1:T(8,128)} %fusion.47, f32[1024,1600]{0,1:T(8,128)} %fusion.46), kind=kLoop, calls=%fused_computation.1 | loop fusion | flops 2621440 | bytes 20971520 | tf_op jit(solution)/shard_map/concatenate | solution.py:861
  168.1 11.5 %copy.77 = f32[1024,2560]{1,0:T(8,128)} copy(f32[1024,2560]{0,1:T(8,128)} %pad_maximum_fusion) | data formatting | bytes 20971520 | tf_op jit(solution)/shard_map/concatenate | solution.py:861
  179.7 4.4 %fusion.6 = bf16[16,32,2560]{2,1,0:T(8,128)(2,1)} fusion(f32[16,2,32,2560]{3,2,1,0:T(8,128)} %bitcast.170, s32[]{:T(128)S(6)} %select_n.92), kind=kLoop, calls=%fused_computation.14 | loop fusion | bytes 5242884 | tf_op jit(solution)/shard_map/convert_element_type | solution.py:868
  184.4 3.4 convolution_convert_fusion.2
  187.8 3.0 copy.79
  190.8 2.2 convolution_convert_fusion
  193.9 2.7 pad_maximum_fusion.1.refs_1_
  198.6 1.9 reshape.332
  201.9 36.7 %all-gather.1 = f32[32,2,960]{2,1,0:T(2,128)} all-gather(f32[1,2,960]{2,1,0:T(2,128)S(1)} %maximum_bitcast_fusion.8), channel_id=2, replica_groups=mesh['fsdp'=32] {'fsdp'}, dimensions={0}, use_global_device_ids=true | all-gather | bytes 253440 | tf_op jit(solution)/shard_map/all_gather | solution.py:882
  240.2 1.9 fusion.36
  242.2 4.1 %fusion.1.refs_0_ = bf16[16,32,2560]{2,1,0:T(8,128)(2,1)S(1)} fusion(bf16[16,32,2560]{2,1,0:T(8,128)(2,1)} %collective-permute-done.6, f32[16,2,32,2560]{3,2,1,0:T(8,128)} %bitcast.171, s32[]{:T(128)S(6)} %select_n.91), kind=kLoop, calls=%fused_computation.6 | loop fusion | flops 3932160 | bytes 10485764 | tf_op jit(solution)/shard_map/convert_element_type | solution.py:868
  246.2 116.2 %scatter_chips.1 = (bf16[32,2560]{1,0:T(8,128)(2,1)S(1)}, bf16[128,1280]{1,0:T(8,128)(2,1)S(1)}, bf16[80,960]{1,0:T(8,128)(2,1)S(1)}) custom-call(bf16[16,32,2560]{2,1,0:T(8,128)(2,1)S(1)} %fusion.1.refs_0_, bf16[16,128,1280]{2,1,0:T(8,128)(2,1)} %pad_maximum_fusion.1.refs_1_, bf16[16,80,960]{2,1,0:T(8,128)(2,1)S(1)} %bitcast.168), custom_call_target="tpu_custom_call" | custom-call | tf_op jit(solution)/shard_map/scatter_chips/pallas_call | solution.py:645
  363.5 2.2 collective-permute-start.7
  (211 shorter events, 50.1 us)
Async XLA Ops:
  0.6 5.4 %copy-start.30 = (bf16[28800]{0:T(1024)(128)(2,1)S(1)}, bf16[28800]{0:T(1024)(128)(2,1)}, u32[]{:S(2)}) copy-start(bf16[28800]{0:T(1024)(128)(2,1)} %param.17) | copy-start | bytes 172804
  0.7 5.5 %copy-start.36 = (bf16[9600]{0:T(1024)(128)(2,1)S(1)}, bf16[9600]{0:T(1024)(128)(2,1)}, u32[]{:S(2)}) copy-start(bf16[9600]{0:T(1024)(128)(2,1)} %param.18) | copy-start | bytes 57604
  0.7 5.6 %copy-start.37 = (bf16[9600]{0:T(1024)(128)(2,1)S(1)}, bf16[9600]{0:T(1024)(128)(2,1)}, u32[]{:S(2)}) copy-start(bf16[9600]{0:T(1024)(128)(2,1)} %param.19) | copy-start | bytes 57604
  0.7 5.7 %copy-start.31 = (bf16[28800]{0:T(1024)(128)(2,1)S(1)}, bf16[28800]{0:T(1024)(128)(2,1)}, u32[]{:S(2)}) copy-start(bf16[28800]{0:T(1024)(128)(2,1)} %param.20) | copy-start | bytes 172804
  0.7 5.8 %copy-start.25 = (bf16[76800]{0:T(1024)(128)(2,1)S(1)}, bf16[76800]{0:T(1024)(128)(2,1)}, u32[]{:S(2)}) copy-start(bf16[76800]{0:T(1024)(128)(2,1)} %param.23) | copy-start | bytes 460804
  4.1 99.0 %copy-start.49 = (s32[64]{0:T(128)S(1)}, s32[64]{0:T(128)}, u32[]{:S(2)}) copy-start(s32[64]{0:T(128)} %param.16) | copy-start | bytes 772
  4.1 100.9 %copy-start.48 = (s32[64]{0:T(128)S(1)}, s32[64]{0:T(128)}, u32[]{:S(2)}) copy-start(s32[64]{0:T(128)} %param.15) | copy-start | bytes 772
  4.1 104.8 %copy-start.14 = (bf16[128,960]{0,1:T(8,128)(2,1)S(1)}, bf16[128,960]{0,1:T(8,128)(2,1)}, u32[]{:S(2)}) copy-start(bf16[128,960]{0,1:T(8,128)(2,1)} %param.14) | copy-start | bytes 737284
  4.1 105.6 %copy-start.1 = (bf16[128,960]{0,1:T(8,128)(2,1)S(1)}, bf16[128,960]{0,1:T(8,128)(2,1)}, u32[]{:S(2)}) copy-start(bf16[128,960]{0,1:T(8,128)(2,1)} %param.13) | copy-start | bytes 737284
  4.1 105.7 %copy-start.34 = (f32[960]{0:T(1024)S(1)}, f32[960]{0:T(1024)}, u32[]{:S(2)}) copy-start(f32[960]{0:T(1024)} %param.24) | copy-start | bytes 11524
  5.3 2.9 collective-permute-start
  101.2 11.6 %collective-permute-start.1 = (bf16[16,32,2560]{2,1,0:T(8,128)(2,1)}, bf16[16,32,2560]{2,1,0:T(8,128)(2,1)S(1)}, u32[]{:S(2)}, u32[]{:S(2)}) collective-permute-start(bf16[16,32,2560]{2,1,0:T(8,128)(2,1)} %get-tuple-element.17), channel_id=1, source_target_pairs={{0,1},{1,0},{2,3},{3,2},{4,5},{5,4},{6,7},{7,6},{8,9},{9,8},{10,11... | collective-permute-start | bytes 7864328 | tf_op jit(solution)/shard_map/ppermute | solution.py:706
  109.7 23.1 %collective-permute-start.4 = (bf16[128,960]{0,1:T(8,128)(2,1)}, bf16[128,960]{0,1:T(8,128)(2,1)}, u32[]{:S(2)}, u32[]{:S(2)}) collective-permute-start(bf16[128,960]{0,1:T(8,128)(2,1)} %fusion.42), channel_id=1, source_target_pairs={{0,1},{1,0},{2,3},{3,2},{4,5},{5,4},{6,7},{7,6},{8,9},{9,8},{10,11... | collective-permute-start | bytes 737288 | tf_op jit(solution)/shard_map/ppermute | solution.py:706
  109.9 7.2 %copy-start.43 = (f32[128]{0:T(128)}, f32[128]{0:T(128)S(1)}, u32[]{:S(2)}) copy-start(f32[128]{0:T(128)S(1)} %add_rsqrt_fusion.1) | copy-start | bytes 1540
  111.8 5.8 %copy-start.8 = (bf16[128,32,32]{0,2,1:T(8,128)(2,1)}, bf16[128,32,32]{0,2,1:T(8,128)(2,1)S(1)}, u32[]{:S(2)}) copy-start(bf16[128,32,32]{0,2,1:T(8,128)(2,1)S(1)} %pad.18) | copy-start | bytes 786436
  112.7 9.0 %copy-start.39 = (pred[128,128]{0,1:T(8,128)(4,1)}, pred[128,128]{0,1:T(8,128)(4,1)S(1)}, u32[]{:S(2)}) copy-start(pred[128,128]{0,1:T(8,128)(4,1)S(1)} %fusion.50) | copy-start | bytes 49156
  123.0 4.5 %copy-start.10 = (bf16[128,32,32]{0,2,1:T(8,128)(2,1)}, bf16[128,32,32]{0,2,1:T(8,128)(2,1)S(1)}, u32[]{:S(2)}) copy-start(bf16[128,32,32]{0,2,1:T(8,128)(2,1)S(1)} %pad.21) | copy-start | bytes 786436
  127.6 3.4 collective-permute-start.2
  138.0 2.5 collective-permute-start.5
  140.0 2.3 collective-permute-start.3
  179.6 4.8 %copy-start.5 = (bf16[256,1280]{1,0:T(8,128)(2,1)S(1)}, bf16[256,1280]{1,0:T(8,128)(2,1)}, u32[]{:S(2)}) copy-start(bf16[256,1280]{1,0:T(8,128)(2,1)} %copy-done.4) | copy-start | bytes 1966084
  184.0 58.1 %collective-permute-start.6 = (bf16[16,32,2560]{2,1,0:T(8,128)(2,1)}, bf16[16,32,2560]{2,1,0:T(8,128)(2,1)}, u32[]{:S(2)}, u32[]{:S(2)}) collective-permute-start(bf16[16,32,2560]{2,1,0:T(8,128)(2,1)} %fusion.6), channel_id=1, source_target_pairs={{0,1},{1,0},{2,3},{3,2},{4,5},{5,4},{6,7},{7,6},{8,9},{9,8},{10,11... | collective-permute-start | bytes 7864328 | tf_op jit(solution)/shard_map/ppermute | solution.py:706
  196.7 5.1 %copy-start.38 = (f32[960]{0:T(1024)S(1)}, f32[960]{0:T(1024)}, u32[]{:S(2)}) copy-start(f32[960]{0:T(1024)} %get-tuple-element.23) | copy-start | bytes 11524
  363.5 5.6 %collective-permute-start.7 = (bf16[2,32,1280]{2,0,1:T(2,128)(2,1)S(1)}, bf16[2,32,1280]{2,0,1:T(2,128)(2,1)S(1)}, u32[]{:S(2)}, u32[]{:S(2)}) collective-permute-start(bf16[2,32,1280]{2,0,1:T(2,128)(2,1)S(1)} %bitcast.221), channel_id=1, source_target_pairs={{0,1},{1,0},{2,3},{3,2},{4,5},{5,4},{6,7},{7,6},{8,9},{9,8},{10,11... | collective-permute-start | bytes 491528 | tf_op jit(solution)/shard_map/ppermute | solution.py:706
  (36 other events, 81.8 us)

commit v3 on v2

--- a/solution.py
+++ b/solution.py
@@ -328,14 +328,15 @@
 def greet_neighbours(core, z, y, x):
     barrier = pltpu.get_barrier_semaphore()
 
-    def greet(z_to, y_to, x_to):
+    def greet(z_to, y_to, x_to, core_to=core):
         pl.semaphore_signal(
             barrier,
             inc=1,
-            device_id=(chip_number(z_to, y_to, x_to) * 2 + core,),
+            device_id=(chip_number(z_to, y_to, x_to) * 2 + core_to,),
             device_id_type=MESH,
         )
 
+    greet(z, y, x, 1 - core)
     greet(z, 1 - y, x)
     greet(z, y, 1 - x)
 
@@ -347,7 +348,7 @@
     def _():
         greet(z + 1, y, x)
 
-    pl.semaphore_wait(barrier, jnp.where((z > 0) & (z < LINE - 1), 4, 3))
+    pl.semaphore_wait(barrier, jnp.where((z > 0) & (z < LINE - 1), 5, 4))
 
 
 def half_rows(refs, half):
@@ -365,20 +366,34 @@
 
 def gather_kernel(*refs):
     ins, outs = refs[0:3], refs[3:6]
-    own_sem, recv_sem, up_sem, down_sem, first_sem, second_sem = refs[6:]
+    own_sem, recv_sem, up_sem, down_sem, first_sem, second_sem, pair_send, pair_recv = refs[6:]
     core, z, y, x = chip_place()
     greet_neighbours(core, z, y, x)
     me = chip_number(z, y, x)
     rows = [half_rows(ins, half) for half in range(2)]
     pending = []
 
+    def out_at(i, source, span, side=core):
+        return outs[0].at[source, side, span] if i == 0 else outs[i].at[source, span]
+
+    def to_pair(half, source, is_own):
+        span = rows[half][0]
+        return pltpu.make_async_remote_copy(
+            src_ref=ins[0].at[span] if is_own else out_at(0, source, span),
+            dst_ref=out_at(0, source, span),
+            send_sem=pair_send.at[half, source],
+            recv_sem=pair_recv.at[half, source],
+            device_id=(me * 2 + 1 - core,),
+            device_id_type=MESH,
+        )
+
     def send(half, source, is_own, sem, slot, target):
         for i in range(3):
             span = rows[half][i]
-            src = ins[i].at[span] if is_own else outs[i].at[source, span]
+            src = ins[i].at[span] if is_own else out_at(i, source, span)
             copy = pltpu.make_async_remote_copy(
                 src_ref=src,
-                dst_ref=outs[i].at[source, span],
+                dst_ref=out_at(i, source, span),
                 send_sem=sem.at[half, i, slot],
                 recv_sem=recv_sem.at[half, i, source],
                 device_id=(target * 2 + core,),
@@ -400,15 +415,16 @@
 
     def receive(half, source):
         for i in range(3):
-            view = outs[i].at[source, rows[half][i]]
+            view = out_at(i, source, rows[half][i])
             pltpu.make_async_remote_copy(
                 src_ref=view,
                 dst_ref=view,
                 send_sem=own_sem.at[i],
                 recv_sem=recv_sem.at[half, i, source],
-                device_id=(me * 2 + core,),
+                device_id=(me * 2 + 1 - core,),
                 device_id_type=MESH,
             ).wait_recv()
+        to_pair(half, source, False).start()
 
     def across(half, place):
         return (1 - y, x) if (half == 0) == (place == 0) else (y, 1 - x)
@@ -442,9 +458,13 @@
             ok, half, source, False, second_sem, LINE + z_from, chip_number(z, *across(half, 1))
         )
 
-    local = [pltpu.make_async_copy(ins[i], outs[i].at[me], own_sem.at[i]) for i in range(3)]
+    whole = [pl.ds(0, ref.shape[0]) for ref in ins]
+    local = [
+        pltpu.make_async_copy(ins[i], out_at(i, me, whole[i]), own_sem.at[i]) for i in range(3)
+    ]
     for half in range(2):
         spread_line(half, 0)
+        to_pair(half, me, True).start()
     for copy in local:
         copy.start()
     for distance in range(LINE):
@@ -465,15 +485,28 @@
             receive(half, chip_number(z_from, 1 - y, 1 - x))
     for copy in local:
         copy.wait()
+    for half in range(2):
+        span = rows[half][0]
+        for source in range(CHIPS):
+            view = out_at(0, source, span, 1 - core)
+            pltpu.make_async_remote_copy(
+                src_ref=view,
+                dst_ref=view,
+                send_sem=pair_send.at[half, source],
+                recv_sem=pair_recv.at[half, source],
+                device_id=(me * 2 + 1 - core,),
+                device_id_type=MESH,
+            ).wait_recv()
+            to_pair(half, source, False).wait_send()
     for condition, (half, source, is_own, sem, slot, target) in pending:
 
         def finish():
             for i in range(3):
                 span = rows[half][i]
-                src = ins[i].at[span] if is_own else outs[i].at[source, span]
+                src = ins[i].at[span] if is_own else out_at(i, source, span)
                 pltpu.make_async_remote_copy(
                     src_ref=src,
-                    dst_ref=outs[i].at[source, span],
+                    dst_ref=out_at(i, source, span),
                     send_sem=sem.at[half, i, slot],
                     recv_sem=recv_sem.at[half, i, source],
                     device_id=(target * 2 + core,),
@@ -490,7 +523,10 @@
     dma = pltpu.SemaphoreType.DMA
     return pl.pallas_call(
         gather_kernel,
-        out_shape=[jax.ShapeDtypeStruct((CHIPS,) + item.shape, item.dtype) for item in blocks],
+        out_shape=[
+            jax.ShapeDtypeStruct((CHIPS,) + extra + item.shape, item.dtype)
+            for item, extra in zip(blocks, ((2,), (), ()))
+        ],
         in_specs=[pl.BlockSpec(memory_space=pl.ANY)] * 3,
         out_specs=[pl.BlockSpec(memory_space=pl.ANY)] * 3,
         scratch_shapes=[
@@ -500,6 +536,8 @@
             dma((2, 3, LINE)),
             dma((2, 3, LINE)),
             dma((2, 3, 2 * LINE)),
+            dma((2, CHIPS)),
+            dma((2, CHIPS)),
         ],
         compiler_params=pltpu.CompilerParams(collective_id=1, has_side_effects=True),
         name="gather_chips",
@@ -507,9 +545,10 @@
 
 
 def scatter_kernel(*refs):
-    ins, outs = refs[0:3], refs[3:6]
-    far, side, low, high = refs[6:9], refs[9:12], refs[12:15], refs[15:18]
-    far_send, far_recv, side_send, side_recv, up_send, low_recv, down_send, high_recv = refs[18:]
+    ins, gains, outs, gains_out = refs[0:3], refs[3], refs[4:7], refs[7]
+    far, side, low, high = refs[8:11], refs[11:14], refs[14:17], refs[17:20]
+    far_send, far_recv, side_send, side_recv, up_send, low_recv, down_send, high_recv = refs[20:28]
+    gain_sum, gain_got, gain_line, gain_send, gain_recv, line_up, line_down, line_recv = refs[28:]
     core, z, y, x = chip_place()
     greet_neighbours(core, z, y, x)
     rows = [half_rows(outs, half) for half in range(2)]
@@ -607,6 +646,63 @@
                 inside(step), half, side, z_to, high, z_to, down_send, high_recv, chip_number(z - 1, y, x)
             )
 
+    me = chip_number(z, y, x)
+    partners = (
+        me * 2 + 1 - core,
+        chip_number(z, y, 1 - x) * 2 + core,
+        chip_number(z, 1 - y, x) * 2 + core,
+    )
+
+    def gain_swap(stage):
+        return pltpu.make_async_remote_copy(
+            src_ref=gains if stage == 0 else gain_sum.at[stage - 1],
+            dst_ref=gain_got.at[stage],
+            send_sem=gain_send.at[stage],
+            recv_sem=gain_recv.at[stage],
+            device_id=(partners[stage],),
+            device_id_type=MESH,
+        )
+
+    def gain_add(stage):
+        gain_swap(stage).wait_recv()
+        before = gains[...] if stage == 0 else gain_sum[stage - 1]
+        total = before + gain_got[stage]
+        if stage < 2:
+            gain_sum[stage] = total
+            gain_swap(stage + 1).start()
+        else:
+            gain_line[z] = total
+
+    def gain_pass(slot, sem, z_to):
+        return pltpu.make_async_remote_copy(
+            src_ref=gain_line.at[slot],
+            dst_ref=gain_line.at[slot],
+            send_sem=sem.at[slot],
+            recv_sem=line_recv.at[slot],
+            device_id=(chip_number(z_to, y, x) * 2 + core,),
+            device_id_type=MESH,
+        )
+
+    def gain_along(step, finish):
+        slot = z + step
+
+        def go(copy):
+            if finish:
+                copy.wait_send()
+            else:
+                copy.start()
+
+        def work():
+            if step != 0 and not finish:
+                gain_pass(slot, line_up, z).wait_recv()
+            if step >= 0:
+                pl.when(z > 0)(lambda: go(gain_pass(slot, line_down, z - 1)))
+            if step <= 0:
+                pl.when(z < LINE - 1)(lambda: go(gain_pass(slot, line_up, z + 1)))
+
+        pl.when(inside(step))(work)
+
+    gain_swap(0).start()
     for distance in reversed(range(LINE)):
         for step in steps_at(distance):
             for half in range(2):
@@ -618,6 +714,7 @@
                 ok = inside(step)
                 send(ok, half, ins, first, far, LINE + z_to, far_send, far_recv, target)
                 send(ok, half, ins, own, far, z_to, far_send, far_recv, target)
+    gain_add(0)
     for distance in (3, 2, 1, 0, -1):
         if distance >= 0:
             for step in steps_at(distance):
@@ -627,6 +724,23 @@
             for step in steps_at(distance + 1):
                 for half in range(2):
                     over_line(half, step)
+        if distance == 3:
+            gain_add(1)
+        elif distance == 2:
+            gain_add(2)
+            gain_along(0, False)
+        else:
+            for step in steps_at(2 - distance):
+                gain_along(step, False)
+    total = gain_line[0]
+    for slot in range(1, LINE):
+        total = total + gain_line[slot]
+    gains_out[...] = total
+    for stage in range(3):
+        gain_swap(stage).wait_send()
+    for distance in range(LINE):
+        for step in steps_at(distance):
+            gain_along(step, True)
     for condition, args in pending:
 
         def finish():
@@ -636,7 +750,7 @@
         pl.when(condition)(finish)
 
 
-def scatter_chips(blocks):
+def scatter_chips(blocks, gains):
     dma = pltpu.SemaphoreType.DMA
 
     def slots(number):
@@ -644,20 +758,31 @@
 
     return pl.pallas_call(
         scatter_kernel,
-        out_shape=[jax.ShapeDtypeStruct(item.shape[1:], item.dtype) for item in blocks],
-        in_specs=[pl.BlockSpec(memory_space=pltpu.VMEM)] * 3,
-        out_specs=[pl.BlockSpec(memory_space=pltpu.VMEM)] * 3,
+        out_shape=[jax.ShapeDtypeStruct(item.shape[1:], item.dtype) for item in blocks]
+        + [jax.ShapeDtypeStruct(gains.shape, gains.dtype)],
+        in_specs=[pl.BlockSpec(memory_space=pltpu.VMEM)] * 4,
+        out_specs=[pl.BlockSpec(memory_space=pltpu.VMEM)] * 4,
         scratch_shapes=slots(2 * LINE)
         + slots(LINE)
         + slots(LINE)
         + slots(LINE)
         + [dma((2, 3, 2 * LINE))] * 2
-        + [dma((2, 3, LINE))] * 6,
+        + [dma((2, 3, LINE))] * 6
+        + [
+            pltpu.VMEM((2,) + gains.shape, gains.dtype),
+            pltpu.VMEM((3,) + gains.shape, gains.dtype),
+            pltpu.VMEM((LINE,) + gains.shape, gains.dtype),
+            dma((3,)),
+            dma((3,)),
+            dma((LINE,)),
+            dma((LINE,)),
+            dma((LINE,)),
+        ],
         compiler_params=pltpu.CompilerParams(
             collective_id=2, has_side_effects=True, vmem_limit_bytes=44 * 1024 * 1024
         ),
         name="scatter_chips",
-    )(*blocks)
+    )(*blocks, gains)
 
 
 def pad_rows(block, spare):
@@ -715,6 +840,15 @@
     def take_core(pair, index):
         return lax.dynamic_index_in_dim(pair, index, axis=0, keepdims=False)
 
+    def row_pair(values):
+        split = values.reshape(row_count, chips, 2, BLOCK)
+        keep = lax.dynamic_index_in_dim(split, core, axis=2, keepdims=False)
+        give = lax.dynamic_index_in_dim(split, 1 - core, axis=2, keepdims=False)
+        return jnp.concatenate([keep, other_core(give)], axis=0).reshape(2 * row_count, chips * BLOCK)
+
+    def token_pair(values):
+        return jnp.concatenate([values, other_core(values)], axis=0)
+
     attention_shard = pad_rows(
         jnp.concatenate(
             [
@@ -732,21 +866,18 @@
     gate_up = jnp.pad(gate_up, ((0, 0), (0, 0), (0, spare), (0, 0)))
     gate_up_other = other_core(take_core(gate_up, 1 - core))
     gate_up_pair = in_core_order(take_core(gate_up, core), gate_up_other, 1)
-    attention_mine, gate_up_all, down_all = gather_chips(
+    attention_all, gate_up_all, down_all = gather_chips(
         [
             attention_shard,
             gate_up_pair.reshape(4 * BLOCK, chips * units),
             down_weight.reshape(units, D),
         ]
     )
-    attention_other = other_core(attention_mine)
     w_gate = gate_up_all[:, : 2 * BLOCK].reshape(count * BLOCK, chips * units)
     w_up = gate_up_all[:, 2 * BLOCK :].reshape(count * BLOCK, chips * units)
     w_down = down_all.reshape(chips * units, D)
 
-    attention_all = in_core_order(attention_mine[:, None], attention_other[:, None], 1).reshape(
-        count * BLOCK, 2 * HEADS * HD + 2 * KV_HEADS * HD
-    )
+    attention_all = attention_all.reshape(count * BLOCK, 2 * HEADS * HD + 2 * KV_HEADS * HD)
     wide_qkv = (HEADS + 2 * KV_HEADS) * HD
     w_qkv = attention_all[:, :wide_qkv]
     w_out = attention_all[:, wide_qkv:]
@@ -761,6 +892,7 @@
     scale_one = rms_scale(inputs)
     normed_one = inputs * scale_one
     low_one = spread((normed_one * attention_gain).astype(jnp.bfloat16), count)
+    low_one_pair = row_pair(low_one)
     qkv = jnp.dot(low_one, w_qkv, preferred_element_type=jnp.float32)
     query_pre = qkv[:, : HEADS * HD].reshape(row_count, HEADS, HD)
     key_pre = qkv[:, HEADS * HD : (HEADS + KV_HEADS) * HD].reshape(row_count, KV_HEADS, HD)
@@ -785,6 +917,7 @@
         "kgij,jkd->ikgd", prob_rows, value_low, preferred_element_type=jnp.float32
     )
     attended_low = spread(attended.reshape(row_count, HEADS * HD).astype(jnp.bfloat16), count)
+    attended_pair = row_pair(attended_low)
     middle = inputs + jnp.dot(attended_low, w_out, preferred_element_type=jnp.float32)
     scale_two = rms_scale(middle)
     normed_two = middle * scale_two
@@ -825,7 +958,7 @@
         scaled_two - normed_two * jnp.mean(scaled_two * normed_two, axis=-1, keepdims=True)
     )
     grad_branch_low = grad_middle.astype(jnp.bfloat16)
-    grad_wout = outer_sum(attended_low, grad_branch_low)
+    grad_wout = outer_sum(attended_pair, token_pair(grad_branch_low)).astype(jnp.bfloat16)
     grad_attended = gather_in(
         times_t(grad_branch_low, w_out).astype(jnp.bfloat16), count, width
     ).reshape(row_count, KV_HEADS, groups, HD)
@@ -857,20 +990,10 @@
         ],
         axis=1,
     )
-    grad_wqkv = outer_sum(low_one, grad_qkv)
+    grad_wqkv = outer_sum(low_one_pair, token_pair(grad_qkv)).astype(jnp.bfloat16)
     grad_attention = jnp.concatenate([grad_wqkv, grad_wout], axis=1).reshape(
-        chips, 2, BLOCK, 2 * HEADS * HD + 2 * KV_HEADS * HD
-    )
-    keep = lax.dynamic_index_in_dim(grad_attention, core, axis=1, keepdims=False)
-    give = lax.dynamic_index_in_dim(grad_attention, 1 - core, axis=1, keepdims=False)
-    attention_sum, gate_up_sum, down_sum = scatter_chips(
-        [
-            (keep + other_core(give.astype(jnp.bfloat16)).astype(jnp.float32)).astype(jnp.bfloat16),
-            grad_gate_up,
-            grad_wdown.reshape(chips, units, D),
-        ]
-    )
-    attention_sum = attention_sum[:width].astype(jnp.float32)
+        chips, BLOCK, 2 * HEADS * HD + 2 * KV_HEADS * HD
+    )
 
     grad_norm_one = gather_in(times_t(grad_qkv, w_qkv), count, width)
     grad_gain_one = jnp.sum(grad_norm_one * normed_one, axis=0)
@@ -878,9 +1001,13 @@
     grad_inputs = grad_middle + scale_one * (
         scaled_one - normed_one * jnp.mean(scaled_one * normed_one, axis=-1, keepdims=True)
     )
-    gain_sums = jnp.sum(
-        lax.all_gather(jnp.stack([grad_gain_one, grad_gain_two]), "fsdp", axis=0), axis=0
-    )
+    gain_rows = jnp.concatenate(
+        [grad_gain_one[None], grad_gain_two[None], jnp.zeros((6, D), jnp.float32)], axis=0
+    )
+    attention_sum, gate_up_sum, down_sum, gain_sums = scatter_chips(
+        [grad_attention, grad_gate_up, grad_wdown.reshape(chips, units, D)], gain_rows
+    )
+    attention_sum = attention_sum[:width].astype(jnp.float32)
 
     gate_up_sum = gate_up_sum.reshape(2, 2, BLOCK, chips * units).transpose(1, 0, 2, 3)
     gate_up_got = other_core(take_core(gate_up_sum, 1 - core))

time: 380 us -> 330 us (0.87)
  blocking collectives: 36.7 us -> 0 us
  other arithmetic: 37.8 us -> 26.5 us
    all_gather x1 -> x0, blocking collectives: 36.7 us -> none  [paired_on_device(): lax.all_gather(jnp.stack([grad_gain_one, grad_gain_two]), 'fsdp', axis=0)]
    concatenate x1, other arithmetic: 10.1 us -> 1.66 us  [paired_on_device(): jnp.concatenate([grad_wqkv, grad_wout], axis=1)]
    concatenate x1, local copies, waits for them, and re-layouts: 11.5 us -> 4.48 us  [paired_on_device(): jnp.concatenate([grad_wqkv, grad_wout], axis=1)]
    pallas_call x1, Pallas kernels: 116 us -> 112 us  [scatter_chips(): pl.pallas_call(scatter_kernel, out_shape=[jax.ShapeDtypeStruct(item.shape...]
    convert_element_type x1 -> x0, local copies, waits for them, and re-layouts: 4.38 us -> none  [paired_on_device(): give.astype(jnp.bfloat16)]
    select_n x2 -> x1, other arithmetic: 5.07 us -> 0.78 us  [in_core_order(): jnp.where(core == 0, jnp.concatenate([mine, theirs], axis=axis), jnp.conc...]
  transfers between devices with their start and end apart: 8 -> 10, of which waited for: 1 -> 0; matrix products, arithmetic and copies ran while one was open for 15% -> 26% of each run, Pallas kernels for 0% -> 30%
where the time goes in v3:
time: 330 us; the launch traced here: 323 us
  Pallas kernels  207 us (63%)
  local copies, waits for them, and re-layouts  43.8 us (13%)
  matrix products  37.6 us (11%)
  other arithmetic  26.5 us (8%)
  starting transfers between devices  4.63 us (1%)
  between operations  3.38 us (1%)
    pallas_call x1, Pallas kernels, scatter_chips(): pl.pallas_call(scatter_kernel, out_shape=[jax.ShapeDtypeStruct(item.shape...  112 us
    pallas_call x1, Pallas kernels, gather_chips(): pl.pallas_call(gather_kernel, out_shape=[jax.ShapeDtypeStruct((CHIPS,) +...  95.8 us
    dot_general x5, matrix products, times_t(): lax.dot_general(left_side, right_side, (((1,), (1,)), ((), ())), preferre...  10.7 us
    dot_general x5, matrix products, outer_sum(): lax.dot_general(left_side, right_side, (((0,), (0,)), ((), ())), preferre...  10.3 us
  transfers between devices with their start and end apart: 10, of which 0 were waited for; matrix products, arithmetic and copies ran while one was open for 26% of the time, Pallas kernels for 30%

profile of v3, /device:TPU:9, one launch (start us, length us, event | category | flops | bytes accessed | tf_op | source)
XLA Modules:
  0.0 323.4 jit_solution(1198458957106041265)
XLA Ops:
  7.9 1.9 fusion.65
  18.1 95.8 %gather_chips.1 = (bf16[16,2,32,2560]{3,2,1,0:T(8,128)(2,1)}, bf16[16,128,1280]{2,1,0:T(8,128)(2,1)}, bf16[16,80,960]{2,1,0:T(8,128)(2,1)}) custom-call(bf16[32,2560]{1,0:T(8,128)(2,1)} %pad.19.refs_0_, bf16[128,1280]{1,0:T(8,128)(2,1)} %bitcast.183, bf16[80,960]{1,0:T(8,128)(2,1)} %reshape.322.refs_2_), custom_call_target="tpu_custom_call" | custom-call | tf_op jit(solution)/shard_map/gather_chips/pallas_call | solution.py:524
  113.9 3.4 %fusion.3 = f32[128,1600]{0,1:T(8,128)S(1)} fusion(bf16[128,1024]{0,1:T(8,128)(2,1)S(1)} %bitcast.185, bf16[1024,2560]{1,0:T(8,128)(2,1)} %bitcast.221), kind=kOutput, calls=%fused_computation.7 | convolution fusion | flops 419430400 | bytes 4489216 | tf_op jit(solution)/shard_map/dot_general | solution.py:896
  120.4 3.5 %multiply_reduce_fusion.3 = (f32[128]{0:T(128)S(1)}, f32[128,960]{0,1:T(8,128)S(1)}) fusion(bf16[128,1024]{0,1:T(8,128)(2,1)S(1)} %bitcast.186, bf16[1024,2560]{1,0:T(8,128)(2,1)} %bitcast.222, bf16[128,960]{0,1:T(8,128)(2,1)S(1)} %copy-done.4), kind=kOutput, calls=%fused_computation.81 | convolution fusion | flops 252149632 | bytes 3097088 | tf_op jit(solution)/shard_map/dot_general | solution.py:921
  125.0 2.9 fusion.83
  138.2 2.6 convolution_convert_fusion
  140.9 2.3 convolution_convert_fusion.1
  143.2 2.3 convolution_convert_fusion.2
  145.5 3.0 copy.58
  148.5 5.4 %pad_maximum_fusion.refs_1_ = bf16[16,128,1280]{2,1,0:T(8,128)(2,1)} fusion(bf16[16,64,1280]{2,1,0:T(8,128)(2,1)} %bitcast.168, bf16[16,64,1280]{2,1,0:T(8,128)(2,1)} %bitcast.169), kind=kLoop, calls=%fused_computation.1 | loop fusion | flops 10485760 | bytes 10485760 | tf_op jit(solution)/shard_map/concatenate | solution.py:944
  153.9 1.9 slice_add_fusion
  155.8 2.0 copy.51
  157.8 1.9 reshape.334
  159.7 2.0 multiply_reduce_fusion.1
  162.2 2.1 fusion.82
  164.3 3.6 %fusion.18 = bf16[128,1024]{1,0:T(8,128)(2,1)} fusion(bf16[128,960]{0,1:T(8,128)(2,1)} %fusion.82, bf16[1024,2560]{1,0:T(8,128)(2,1)} %bitcast.223), kind=kOutput, calls=%fused_computation.32 | convolution fusion | flops 251789312 | bytes 2605056 | tf_op jit(solution)/shard_map/dot_general | solution.py:91
  167.9 1.8 copy.52
  171.4 2.3 fusion.24
  173.8 1.8 multiply_reduce_fusion
  177.1 3.9 %fusion.1 = f32[128,1024]{0,1:T(8,128)} fusion(bf16[1024,2560]{1,0:T(8,128)(2,1)} %bitcast.224, bf16[128,320]{0,1:T(8,128)(2,1)S(1)} %bitcast.212, bf16[128,320]{0,1:T(8,128)(2,1)S(1)} %bitcast.204, bf16[128,960]{0,1:T(8,128)(2,1)S(1)} %bitcast.189), kind=kOutput, calls=%fused_computation.5 | convolution fusion | flops 420659200 | bytes 4341760 | tf_op jit(solution)/shard_map/dot_general | solution.py:91
  181.8 1.9 reshape.338
  185.5 2.8 fusion.41
  193.2 4.5 %copy.57 = bf16[512,2560]{1,0:T(8,128)(2,1)} copy(bf16[512,2560]{0,1:T(8,128)(2,1)} %pad_maximum_fusion.1) | data formatting | bytes 5242880 | tf_op jit(solution)/shard_map/concatenate | solution.py:994
  199.4 111.6 %scatter_chips.1 = (bf16[32,2560]{1,0:T(8,128)(2,1)S(1)}, bf16[128,1280]{1,0:T(8,128)(2,1)S(1)}, bf16[80,960]{1,0:T(8,128)(2,1)S(1)}, f32[8,960]{1,0:T(8,128)S(1)}) custom-call(bf16[16,32,2560]{2,1,0:T(8,128)(2,1)S(1)} %bitcast.164, bf16[16,128,1280]{2,1,0:T(8,128)(2,1)} %pad_maximum_fusion.refs_1_, bf16[16,80,960]{2,1,0:T(8,128)(2,1)S(1)} %bitcast.163, ...), custom_call_target="tpu_custom_call" | custom-call | tf_op jit(solution)/shard_map/scatter_chips/pallas_call | solution.py:759
  (195 shorter events, 52.7 us)
Async XLA Ops:
  0.7 7.3 %copy-start.40 = (s32[64]{0:T(128)S(1)}, s32[64]{0:T(128)}, u32[]{:S(2)}) copy-start(s32[64]{0:T(128)} %param.15) | copy-start | bytes 772
  0.7 11.1 %copy-start.6 = (bf16[128,960]{0,1:T(8,128)(2,1)S(1)}, bf16[128,960]{0,1:T(8,128)(2,1)}, u32[]{:S(2)}) copy-start(bf16[128,960]{0,1:T(8,128)(2,1)} %param.14) | copy-start | bytes 737284
  0.7 11.3 %copy-start.4 = (bf16[128,960]{0,1:T(8,128)(2,1)S(1)}, bf16[128,960]{0,1:T(8,128)(2,1)}, u32[]{:S(2)}) copy-start(bf16[128,960]{0,1:T(8,128)(2,1)} %param.13) | copy-start | bytes 737284
  0.7 11.4 %copy-start.24 = (f32[960]{0:T(1024)S(1)}, f32[960]{0:T(1024)}, u32[]{:S(2)}) copy-start(f32[960]{0:T(1024)} %param.24) | copy-start | bytes 11524
  4.0 10.3 %copy-start.22 = (bf16[28800]{0:T(1024)(128)(2,1)S(1)}, bf16[28800]{0:T(1024)(128)(2,1)}, u32[]{:S(2)}) copy-start(bf16[28800]{0:T(1024)(128)(2,1)} %param.17) | copy-start | bytes 172804
  4.0 10.5 %copy-start.26 = (bf16[9600]{0:T(1024)(128)(2,1)S(1)}, bf16[9600]{0:T(1024)(128)(2,1)}, u32[]{:S(2)}) copy-start(bf16[9600]{0:T(1024)(128)(2,1)} %param.18) | copy-start | bytes 57604
  4.1 10.5 %copy-start.27 = (bf16[9600]{0:T(1024)(128)(2,1)S(1)}, bf16[9600]{0:T(1024)(128)(2,1)}, u32[]{:S(2)}) copy-start(bf16[9600]{0:T(1024)(128)(2,1)} %param.19) | copy-start | bytes 57604
  4.1 10.6 %copy-start.23 = (bf16[28800]{0:T(1024)(128)(2,1)S(1)}, bf16[28800]{0:T(1024)(128)(2,1)}, u32[]{:S(2)}) copy-start(bf16[28800]{0:T(1024)(128)(2,1)} %param.20) | copy-start | bytes 172804
  4.9 10.7 %copy-start.14 = (bf16[76800]{0:T(1024)(128)(2,1)S(1)}, bf16[76800]{0:T(1024)(128)(2,1)}, u32[]{:S(2)}) copy-start(bf16[76800]{0:T(1024)(128)(2,1)} %param.23) | copy-start | bytes 460804
  5.3 12.1 %collective-permute-start = (bf16[2,32,1280]{2,1,0:T(8,128)(2,1)S(1)}, bf16[2,32,1280]{2,1,0:T(8,128)(2,1)S(1)}, u32[]{:S(2)}, u32[]{:S(2)}) collective-permute-start(bf16[2,32,1280]{2,1,0:T(8,128)(2,1)S(1)} %bitcast.208), channel_id=1, source_target_pairs={{0,1},{1,0},{2,3},{3,2},{4,5},{5,4},{6,7},{7,6},{8,9},{9,8},{10,11... | collective-permute-start | bytes 491528 | tf_op jit(solution)/shard_map/ppermute | solution.py:831
  11.9 118.9 %collective-permute-start.3 = (bf16[128,960]{0,1:T(8,128)(2,1)S(1)}, bf16[128,960]{0,1:T(8,128)(2,1)S(1)}, u32[]{:S(2)}, u32[]{:S(2)}) collective-permute-start(bf16[128,960]{0,1:T(8,128)(2,1)S(1)} %fusion.50), channel_id=1, source_target_pairs={{0,1},{1,0},{2,3},{3,2},{4,5},{5,4},{6,7},{7,6},{8,9},{9,8},{10,11... | collective-permute-start | bytes 737288 | tf_op jit(solution)/shard_map/ppermute | solution.py:831
  13.2 176.8 %collective-permute-start.5 = (bf16[128,16,32]{0,2,1:T(8,128)(2,1)}, bf16[128,16,32]{0,2,1:T(8,128)(2,1)}, u32[]{:S(2)}, u32[]{:S(2)}) collective-permute-start(bf16[128,16,32]{0,2,1:T(8,128)(2,1)} %get-tuple-element.53), channel_id=1, source_target_pairs={{0,1},{1,0},{2,3},{3,2},{4,5},{5,4},{6,7},{7,6},{8,9},{9,8},{10,11... | collective-permute-start | bytes 393224 | tf_op jit(solution)/shard_map/ppermute | solution.py:831
  17.3 101.7 %copy-start.29 = (pred[128,128]{0,1:T(8,128)(4,1)}, pred[128,128]{0,1:T(8,128)(4,1)S(1)}, u32[]{:S(2)}) copy-start(pred[128,128]{0,1:T(8,128)(4,1)S(1)} %fusion.60) | copy-start | bytes 49156
  124.8 4.2 %collective-permute-start.1 = (bf16[128,1024]{0,1:T(8,128)(2,1)S(1)}, bf16[128,1024]{0,1:T(8,128)(2,1)S(1)}, u32[]{:S(2)}, u32[]{:S(2)}) collective-permute-start(bf16[128,1024]{0,1:T(8,128)(2,1)S(1)} %bitcast.175), channel_id=1, source_target_pairs={{0,1},{1,0},{2,3},{3,2},{4,5},{5,4},{6,7},{7,6},{8,9},{9,8},{10,11... | collective-permute-start | bytes 786440 | tf_op jit(solution)/shard_map/ppermute | solution.py:831
  128.6 59.7 %collective-permute-start.7 = (bf16[128,16,32]{0,2,1:T(8,128)(2,1)}, bf16[128,16,32]{0,2,1:T(8,128)(2,1)}, u32[]{:S(2)}, u32[]{:S(2)}) collective-permute-start(bf16[128,16,32]{0,2,1:T(8,128)(2,1)} %get-tuple-element.55), channel_id=1, source_target_pairs={{0,1},{1,0},{2,3},{3,2},{4,5},{5,4},{6,7},{7,6},{8,9},{9,8},{10,11... | collective-permute-start | bytes 393224 | tf_op jit(solution)/shard_map/ppermute | solution.py:831
  135.7 18.2 %collective-permute-start.4 = (f32[128,1024]{1,0:T(8,128)}, f32[128,1024]{1,0:T(8,128)}, u32[]{:S(2)}, u32[]{:S(2)}) collective-permute-start(f32[128,1024]{1,0:T(8,128)} %slice.141), channel_id=1, source_target_pairs={{0,1},{1,0},{2,3},{3,2},{4,5},{5,4},{6,7},{7,6},{8,9},{9,8},{10,11... | collective-permute-start | bytes 1572872 | tf_op jit(solution)/shard_map/ppermute | solution.py:831
  137.9 47.5 %collective-permute-start.2 = (f32[128,960]{0,1:T(8,128)}, f32[128,960]{0,1:T(8,128)}, u32[]{:S(2)}, u32[]{:S(2)}) collective-permute-start(f32[128,960]{0,1:T(8,128)} %slice.139), channel_id=1, source_target_pairs={{0,1},{1,0},{2,3},{3,2},{4,5},{5,4},{6,7},{7,6},{8,9},{9,8},{10,11... | collective-permute-start | bytes 1474568 | tf_op jit(solution)/shard_map/ppermute | solution.py:831
  176.6 11.7 %collective-permute-start.8 = (bf16[128,960]{0,1:T(8,128)(2,1)}, bf16[128,960]{0,1:T(8,128)(2,1)}, u32[]{:S(2)}, u32[]{:S(2)}) collective-permute-start(bf16[128,960]{0,1:T(8,128)(2,1)} %fusion.82), channel_id=1, source_target_pairs={{0,1},{1,0},{2,3},{3,2},{4,5},{5,4},{6,7},{7,6},{8,9},{9,8},{10,11... | collective-permute-start | bytes 737288 | tf_op jit(solution)/shard_map/ppermute | solution.py:831
  177.0 8.4 %copy-start.21 = (f32[960]{0:T(1024)S(1)}, f32[960]{0:T(1024)}, u32[]{:S(2)}) copy-start(f32[960]{0:T(1024)} %param.25) | copy-start | bytes 11524
  177.0 8.4 %copy-start.33 = (f32[128]{0:T(128)S(1)}, f32[128]{0:T(128)}, u32[]{:S(2)}) copy-start(f32[128]{0:T(128)} %copy-done.32) | copy-start | bytes 1540
  177.1 8.4 %copy-start.35 = (f32[128]{0:T(128)S(1)}, f32[128]{0:T(128)}, u32[]{:S(2)}) copy-start(f32[128]{0:T(128)} %copy-done.34) | copy-start | bytes 1540
  177.1 8.4 %copy-start.39 = (f32[128]{0:T(128)S(1)}, f32[128]{0:T(128)}, u32[]{:S(2)}) copy-start(f32[128]{0:T(128)} %copy-done.38) | copy-start | bytes 1540
  183.6 6.3 %collective-permute-start.6 = (bf16[128,1600]{0,1:T(8,128)(2,1)}, bf16[128,1600]{0,1:T(8,128)(2,1)S(1)}, u32[]{:S(2)}, u32[]{:S(2)}) collective-permute-start(bf16[128,1600]{0,1:T(8,128)(2,1)} %pad_maximum_fusion.4), channel_id=1, source_target_pairs={{0,1},{1,0},{2,3},{3,2},{4,5},{5,4},{6,7},{7,6},{8,9},{9,8},{10,11... | collective-permute-start | bytes 1228808 | tf_op jit(solution)/shard_map/ppermute | solution.py:831
  314.4 3.3 %collective-permute-start.9 = (bf16[2,32,1280]{2,0,1:T(2,128)(2,1)S(1)}, bf16[2,32,1280]{2,0,1:T(2,128)(2,1)S(1)}, u32[]{:S(2)}, u32[]{:S(2)}) collective-permute-start(bf16[2,32,1280]{2,0,1:T(2,128)(2,1)S(1)} %bitcast.209), channel_id=1, source_target_pairs={{0,1},{1,0},{2,3},{3,2},{4,5},{5,4},{6,7},{7,6},{8,9},{9,8},{10,11... | collective-permute-start | bytes 491528 | tf_op jit(solution)/shard_map/ppermute | solution.py:831
  (29 other events, 99.3 us)

commit v4 on v3

--- a/solution.py
+++ b/solution.py
@@ -710,16 +710,21 @@
                 target = chip_number(z, y_to, x_to)
                 z_to = z + step
                 first = chip_number(z_to, 1 - y, 1 - x)
-                own = chip_number(z_to, y_to, x_to)
                 ok = inside(step)
                 send(ok, half, ins, first, far, LINE + z_to, far_send, far_recv, target)
-                send(ok, half, ins, own, far, z_to, far_send, far_recv, target)
     gain_add(0)
     for distance in (3, 2, 1, 0, -1):
         if distance >= 0:
             for step in steps_at(distance):
                 for half in range(2):
                     over_side(half, step)
+            for step in steps_at(distance):
+                for half in range(2):
+                    target = chip_number(z, *across(half, 1))
+                    own = chip_number(z + step, *across(half, 1))
+                    send(
+                        inside(step), half, ins, own, far, z + step, far_send, far_recv, target
+                    )
         if distance < LINE - 1:
             for step in steps_at(distance + 1):
                 for half in range(2):
@@ -861,20 +866,24 @@
         ),
         spare,
     )
-    gate_up = jnp.stack([gate_weight.reshape(width, chips, 2, units), up_weight.reshape(width, chips, 2, units)])
-    gate_up = gate_up.transpose(3, 0, 1, 2, 4).reshape(2, 2, width, chips * units)
-    gate_up = jnp.pad(gate_up, ((0, 0), (0, 0), (0, spare), (0, 0)))
+    gate_up = jnp.concatenate(
+        [
+            item.reshape(width, chips, 2, units).transpose(2, 0, 1, 3).reshape(2, width, chips * units)
+            for item in (gate_weight, up_weight)
+        ],
+        axis=2,
+    )
+    gate_up = jnp.pad(gate_up, ((0, 0), (0, spare), (0, 0)))
     gate_up_other = other_core(take_core(gate_up, 1 - core))
-    gate_up_pair = in_core_order(take_core(gate_up, core), gate_up_other, 1)
+    gate_up_pair = in_core_order(take_core(gate_up, core), gate_up_other, 0)
     attention_all, gate_up_all, down_all = gather_chips(
         [
             attention_shard,
-            gate_up_pair.reshape(4 * BLOCK, chips * units),
+            gate_up_pair,
             down_weight.reshape(units, D),
         ]
     )
-    w_gate = gate_up_all[:, : 2 * BLOCK].reshape(count * BLOCK, chips * units)
-    w_up = gate_up_all[:, 2 * BLOCK :].reshape(count * BLOCK, chips * units)
+    w_gate_up = gate_up_all.reshape(count * BLOCK, 2 * chips * units)
     w_down = down_all.reshape(chips * units, D)
 
     attention_all = attention_all.reshape(count * BLOCK, 2 * HEADS * HD + 2 * KV_HEADS * HD)
@@ -924,8 +933,9 @@
     low_two = spread((normed_two * feedforward_gain).astype(jnp.bfloat16), count)
     low_two_both = jnp.concatenate([low_two, other_core(low_two)], axis=0)
 
-    gate_pre = jnp.dot(low_two_both, w_gate, preferred_element_type=jnp.float32)
-    upward = jnp.dot(low_two_both, w_up, preferred_element_type=jnp.float32)
+    gate_and_up = jnp.dot(low_two_both, w_gate_up, preferred_element_type=jnp.float32)
+    gate_pre = gate_and_up[:, : chips * units]
+    upward = gate_and_up[:, chips * units :]
     sigmoid_gate = jax.nn.sigmoid(gate_pre)
     silu_gate = gate_pre * sigmoid_gate
     hidden_low = (silu_gate * upward).astype(jnp.bfloat16)
@@ -939,16 +949,13 @@
     grad_gate = (
         grad_hidden * upward * sigmoid_gate * (1.0 + gate_pre * (1.0 - sigmoid_gate))
     ).astype(jnp.bfloat16)
-    grad_wgate = outer_sum(low_two_both, grad_gate).astype(jnp.bfloat16)
-    grad_wup = outer_sum(low_two_both, grad_up).astype(jnp.bfloat16)
-    grad_gate_up = jnp.concatenate(
-        [
-            grad_wgate.reshape(chips, 2 * BLOCK, chips * units),
-            grad_wup.reshape(chips, 2 * BLOCK, chips * units),
-        ],
-        axis=1,
-    )
-    grad_norm_both = times_t(grad_gate, w_gate) + times_t(grad_up, w_up)
+    grad_both = jnp.concatenate([grad_gate, grad_up], axis=1)
+    grad_gate_up = (
+        outer_sum(low_two_both, grad_both)
+        .astype(jnp.bfloat16)
+        .reshape(chips, 2 * BLOCK, 2 * chips * units)
+    )
+    grad_norm_both = times_t(grad_both, w_gate_up)
     grad_norm_two = gather_in(
         grad_norm_both[:row_count] + other_core(grad_norm_both[row_count:]), count, width
     )
@@ -1009,11 +1016,11 @@
     )
     attention_sum = attention_sum[:width].astype(jnp.float32)
 
-    gate_up_sum = gate_up_sum.reshape(2, 2, BLOCK, chips * units).transpose(1, 0, 2, 3)
+    gate_up_sum = gate_up_sum.reshape(2, BLOCK, 2 * chips * units)
     gate_up_got = other_core(take_core(gate_up_sum, 1 - core))
     gate_up_kept = take_core(gate_up_sum, core)
-    halves = in_core_order(gate_up_kept[None], gate_up_got[None], 0)[:, :, :width]
-    halves = halves.reshape(2, 2, width, chips, units).transpose(1, 2, 3, 0, 4).astype(jnp.float32)
+    halves = in_core_order(gate_up_kept[None], gate_up_got[None], 0)[:, :width]
+    halves = halves.reshape(2, width, 2, chips, units).transpose(2, 1, 3, 0, 4).astype(jnp.float32)
     edge_key, edge_value = HEADS * HD, (HEADS + KV_HEADS) * HD
     return (
         layer_out,

time: 330 us -> 305 us (0.924); the launches traced: 323 us -> 304 us
  Pallas kernels: 207 us -> 192 us
  other arithmetic: 26.5 us -> 21.2 us
  matrix products: 37.6 us -> 41.7 us
    pallas_call x1, Pallas kernels: 112 us -> 96.2 us  [scatter_chips(): pl.pallas_call(scatter_kernel, out_shape=[jax.ShapeDtypeStruct(item.shape...]
    concatenate x1, other arithmetic: 5.43 us -> 0.27 us  [paired_on_device(): jnp.concatenate([item.reshape(width, chips, 2, units).transpose(2, 0, 1,...]
    dot_general x5 -> x4, matrix products: 10.3 us -> 9.23 us  [outer_sum(): lax.dot_general(left_side, right_side, (((0,), (0,)), ((), ())), preferre...]
    dot_general x5 -> x4, matrix products: 10.7 us -> 10.6 us  [times_t(): lax.dot_general(left_side, right_side, (((1,), (1,)), ((), ())), preferre...]
  transfers between devices with their start and end apart: 10 -> 10, of which waited for: 0 -> 0; matrix products, arithmetic and copies ran while one was open for 26% -> 24% of each run, Pallas kernels for 30% -> 0%
where the time goes in v4:
time: 305 us; the launch traced here: 304 us
  Pallas kernels  192 us (63%)
  matrix products  41.7 us (14%)
  local copies, waits for them, and re-layouts  41.1 us (13%)
  other arithmetic  21.2 us (7%)
  starting transfers between devices  4.57 us (1%)
    pallas_call x1, Pallas kernels, scatter_chips(): pl.pallas_call(scatter_kernel, out_shape=[jax.ShapeDtypeStruct(item.shape...  96.2 us
    pallas_call x1, Pallas kernels, gather_chips(): pl.pallas_call(gather_kernel, out_shape=[jax.ShapeDtypeStruct((CHIPS,) +...  95.8 us
    dot_general x4, matrix products, times_t(): lax.dot_general(left_side, right_side, (((1,), (1,)), ((), ())), preferre...  10.6 us
    dot_general x4, matrix products, outer_sum(): lax.dot_general(left_side, right_side, (((0,), (0,)), ((), ())), preferre...  9.23 us
  transfers between devices with their start and end apart: 10, of which 0 were waited for; matrix products, arithmetic and copies ran while one was open for 24% of the time, Pallas kernels for 0%

profile of v4, /device:TPU:9, one launch (start us, length us, event | category | flops | bytes accessed | tf_op | source)
XLA Modules:
  0.0 303.6 jit_solution(5158918064710311055)
XLA Ops:
  8.0 1.9 fusion.71
  16.1 95.8 %gather_chips.1 = (bf16[16,2,32,2560]{3,2,1,0:T(8,128)(2,1)}, bf16[16,64,2560]{2,1,0:T(8,128)(2,1)}, bf16[16,80,960]{2,1,0:T(8,128)(2,1)}) custom-call(bf16[32,2560]{1,0:T(8,128)(2,1)} %pad.19.refs_0_, bf16[64,2560]{1,0:T(8,128)(2,1)} %maximum_select_fusion.refs_1_, bf16[80,960]{1,0:T(8,128)(2,1)} %reshape.320.refs_2_), custom_call_target="tpu_custom_call" | custom-call | tf_op jit(solution)/shard_map/gather_chips/pallas_call | solution.py:524
  111.9 3.4 %fusion.3 = f32[128,1600]{0,1:T(8,128)S(1)} fusion(bf16[128,1024]{0,1:T(8,128)(2,1)S(1)} %bitcast.171, bf16[1024,2560]{1,0:T(8,128)(2,1)} %bitcast.208), kind=kOutput, calls=%fused_computation.5 | convolution fusion | flops 419430400 | bytes 4489216 | tf_op jit(solution)/shard_map/dot_general | solution.py:905
  118.4 3.6 %multiply_reduce_fusion.3 = (f32[128]{0:T(128)S(1)}, f32[128,960]{0,1:T(8,128)S(1)}) fusion(bf16[128,1024]{0,1:T(8,128)(2,1)S(1)} %bitcast.173, bf16[1024,2560]{1,0:T(8,128)(2,1)} %bitcast.209, bf16[128,960]{0,1:T(8,128)(2,1)S(1)} %copy-done.2), kind=kOutput, calls=%fused_computation.81 | convolution fusion | flops 252149632 | bytes 3097088 | tf_op jit(solution)/shard_map/dot_general | solution.py:930
  126.2 4.2 %fusion.54 = f32[256,2560]{1,0:T(8,128)S(1)} fusion(bf16[1024,2560]{1,0:T(8,128)(2,1)} %bitcast.158, bf16[128,1024]{0,1:T(8,128)(2,1)S(1)} %collective-permute-done.1, bf16[128,1024]{0,1:T(8,128)(2,1)S(1)} %bitcast.166), kind=kOutput, calls=%fused_computation.84 | convolution fusion | flops 1343225856 | bytes 8388608 | tf_op jit(solution)/shard_map/dot_general | solution.py:936
  134.7 2.2 convolution_convert_fusion.1
  137.0 3.0 copy.57
  140.0 3.2 %fusion.95 = f32[256,960]{0,1:T(8,128)S(1)} fusion(bf16[256,1280]{1,0:T(8,128)(2,1)} %copy-done.4, bf16[1280,960]{1,0:T(8,128)(2,1)} %bitcast.163), kind=kOutput, calls=%fused_computation.169 | convolution fusion | flops 629145600 | bytes 4096000 | tf_op jit(solution)/shard_map/dot_general | solution.py:942
  145.2 3.9 %convolution_convert_fusion = bf16[1024,2560]{1,0:T(8,128)(2,1)} fusion(bf16[256,1280]{1,0:T(8,128)(2,1)S(1)} %copy-done.18, bf16[256,1280]{1,0:T(8,128)(2,1)S(1)} %copy-done.16, bf16[128,1024]{0,1:T(8,128)(2,1)S(1)} %copy-done.9, bf16[128,1024]{0,1:T(8,128)(2,1)S(1)} %bitcast.167), kind=kOutput, calls=%fused_computation.1 | convolution fusion | flops 1348468736 | bytes 7077888 | tf_op jit(solution)/shard_map/dot_general | solution.py:85
  149.1 1.9 slice_add_fusion
  151.0 2.0 copy.50
  153.0 1.9 reshape.331
  154.9 2.0 multiply_reduce_fusion.1
  157.4 2.1 fusion.89
  159.5 3.6 %fusion.18 = bf16[128,1024]{1,0:T(8,128)(2,1)} fusion(bf16[128,960]{0,1:T(8,128)(2,1)} %fusion.89, bf16[1024,2560]{1,0:T(8,128)(2,1)} %bitcast.210), kind=kOutput, calls=%fused_computation.30 | convolution fusion | flops 251789312 | bytes 2605056 | tf_op jit(solution)/shard_map/dot_general | solution.py:91
  163.1 1.8 copy.51
  169.9 2.4 fusion.24
  173.7 3.9 %fusion.1 = f32[128,1024]{0,1:T(8,128)} fusion(bf16[1024,2560]{1,0:T(8,128)(2,1)} %bitcast.211, bf16[128,320]{0,1:T(8,128)(2,1)} %bitcast.199, bf16[128,320]{0,1:T(8,128)(2,1)S(1)} %bitcast.192, bf16[128,960]{0,1:T(8,128)(2,1)S(1)} %bitcast.176), kind=kOutput, calls=%fused_computation.3 | convolution fusion | flops 420659200 | bytes 4341760 | tf_op jit(solution)/shard_map/dot_general | solution.py:91
  178.6 1.9 reshape.335
  182.2 2.8 fusion.44
  189.9 4.4 %copy.56 = bf16[512,2560]{1,0:T(8,128)(2,1)} copy(bf16[512,2560]{0,1:T(8,128)(2,1)} %pad_maximum_fusion) | data formatting | bytes 5242880 | tf_op jit(solution)/shard_map/concatenate | solution.py:1001
  194.3 1.7 copy-done
  196.0 96.2 %scatter_chips.1 = (bf16[32,2560]{1,0:T(8,128)(2,1)S(1)}, bf16[64,2560]{1,0:T(8,128)(2,1)S(1)}, bf16[80,960]{1,0:T(8,128)(2,1)S(1)}, f32[8,960]{1,0:T(8,128)S(1)}) custom-call(bf16[16,32,2560]{2,1,0:T(8,128)(2,1)S(1)} %bitcast.155, bf16[16,64,2560]{2,1,0:T(8,128)(2,1)} %bitcast.157, bf16[16,80,960]{2,1,0:T(8,128)(2,1)S(1)} %bitcast.154, ...), custom_call_target="tpu_custom_call" | custom-call | tf_op jit(solution)/shard_map/scatter_chips/pallas_call | solution.py:764
  292.5 1.8 collective-permute-start.9
  (214 shorter events, 49.0 us)
Async XLA Ops:
  0.7 11.2 %copy-start.33 = (f32[960]{0:T(1024)S(1)}, f32[960]{0:T(1024)}, u32[]{:S(2)}) copy-start(f32[960]{0:T(1024)} %param.24) | copy-start | bytes 11524
  2.4 10.0 %copy-start.31 = (bf16[28800]{0:T(1024)(128)(2,1)S(1)}, bf16[28800]{0:T(1024)(128)(2,1)}, u32[]{:S(2)}) copy-start(bf16[28800]{0:T(1024)(128)(2,1)} %param.17) | copy-start | bytes 172804
  2.5 10.1 %copy-start.32 = (bf16[28800]{0:T(1024)(128)(2,1)S(1)}, bf16[28800]{0:T(1024)(128)(2,1)}, u32[]{:S(2)}) copy-start(bf16[28800]{0:T(1024)(128)(2,1)} %param.20) | copy-start | bytes 172804
  2.5 10.2 %copy-start.35 = (bf16[9600]{0:T(1024)(128)(2,1)S(1)}, bf16[9600]{0:T(1024)(128)(2,1)}, u32[]{:S(2)}) copy-start(bf16[9600]{0:T(1024)(128)(2,1)} %param.18) | copy-start | bytes 57604
  2.5 10.3 %copy-start.36 = (bf16[9600]{0:T(1024)(128)(2,1)S(1)}, bf16[9600]{0:T(1024)(128)(2,1)}, u32[]{:S(2)}) copy-start(bf16[9600]{0:T(1024)(128)(2,1)} %param.19) | copy-start | bytes 57604
  2.5 10.4 %copy-start.25 = (bf16[76800]{0:T(1024)(128)(2,1)S(1)}, bf16[76800]{0:T(1024)(128)(2,1)}, u32[]{:S(2)}) copy-start(bf16[76800]{0:T(1024)(128)(2,1)} %param.23) | copy-start | bytes 460804
  5.2 10.1 %collective-permute-start = (bf16[32,2560]{1,0:T(8,128)(2,1)S(1)}, bf16[32,2560]{1,0:T(8,128)(2,1)S(1)}, u32[]{:S(2)}, u32[]{:S(2)}) collective-permute-start(bf16[32,2560]{1,0:T(8,128)(2,1)S(1)} %bitcast.196), channel_id=1, source_target_pairs={{0,1},{1,0},{2,3},{3,2},{4,5},{5,4},{6,7},{7,6},{8,9},{9,8},{10,11... | collective-permute-start | bytes 491528 | tf_op jit(solution)/shard_map/ppermute | solution.py:836
  12.4 104.7 %copy-start.38 = (pred[128,128]{0,1:T(8,128)(4,1)}, pred[128,128]{0,1:T(8,128)(4,1)S(1)}, u32[]{:S(2)}) copy-start(pred[128,128]{0,1:T(8,128)(4,1)S(1)} %fusion.66) | copy-start | bytes 49156
  15.3 107.8 %copy-start.43 = (f32[128]{0:T(128)}, f32[128]{0:T(128)S(1)}, u32[]{:S(2)}) copy-start(f32[128]{0:T(128)S(1)} %compare_convert_fusion) | copy-start | bytes 1540
  115.6 53.0 %copy-start.23 = (bf16[128,5,32]{0,2,1:T(8,128)(2,1)}, bf16[128,5,32]{0,2,1:T(8,128)(2,1)S(1)}, u32[]{:S(2)}) copy-start(bf16[128,5,32]{0,2,1:T(8,128)(2,1)S(1)} %get-tuple-element.56) | copy-start | bytes 122884
  115.6 53.0 %copy-start.24 = (bf16[128,5,32]{0,2,1:T(8,128)(2,1)}, bf16[128,5,32]{0,2,1:T(8,128)(2,1)S(1)}, u32[]{:S(2)}) copy-start(bf16[128,5,32]{0,2,1:T(8,128)(2,1)S(1)} %get-tuple-element.57) | copy-start | bytes 122884
  122.9 3.3 %collective-permute-start.1 = (bf16[128,1024]{0,1:T(8,128)(2,1)S(1)}, bf16[128,1024]{0,1:T(8,128)(2,1)S(1)}, u32[]{:S(2)}, u32[]{:S(2)}) collective-permute-start(bf16[128,1024]{0,1:T(8,128)(2,1)S(1)} %bitcast.165), channel_id=1, source_target_pairs={{0,1},{1,0},{2,3},{3,2},{4,5},{5,4},{6,7},{7,6},{8,9},{9,8},{10,11... | collective-permute-start | bytes 786440 | tf_op jit(solution)/shard_map/ppermute | solution.py:836
  123.2 7.2 %collective-permute-start.3 = (bf16[128,960]{0,1:T(8,128)(2,1)S(1)}, bf16[128,960]{0,1:T(8,128)(2,1)S(1)}, u32[]{:S(2)}, u32[]{:S(2)}) collective-permute-start(bf16[128,960]{0,1:T(8,128)(2,1)S(1)} %fusion.53), channel_id=1, source_target_pairs={{0,1},{1,0},{2,3},{3,2},{4,5},{5,4},{6,7},{7,6},{8,9},{9,8},{10,11... | collective-permute-start | bytes 737288 | tf_op jit(solution)/shard_map/ppermute | solution.py:836
  124.3 62.4 %collective-permute-start.5 = (bf16[128,16,32]{0,2,1:T(8,128)(2,1)}, bf16[128,16,32]{0,2,1:T(8,128)(2,1)}, u32[]{:S(2)}, u32[]{:S(2)}) collective-permute-start(bf16[128,16,32]{0,2,1:T(8,128)(2,1)} %get-tuple-element.51), channel_id=1, source_target_pairs={{0,1},{1,0},{2,3},{3,2},{4,5},{5,4},{6,7},{7,6},{8,9},{9,8},{10,11... | collective-permute-start | bytes 393224 | tf_op jit(solution)/shard_map/ppermute | solution.py:836
  125.8 59.3 %collective-permute-start.7 = (bf16[128,16,32]{0,2,1:T(8,128)(2,1)}, bf16[128,16,32]{0,2,1:T(8,128)(2,1)}, u32[]{:S(2)}, u32[]{:S(2)}) collective-permute-start(bf16[128,16,32]{0,2,1:T(8,128)(2,1)} %get-tuple-element.53), channel_id=1, source_target_pairs={{0,1},{1,0},{2,3},{3,2},{4,5},{5,4},{6,7},{7,6},{8,9},{9,8},{10,11... | collective-permute-start | bytes 393224 | tf_op jit(solution)/shard_map/ppermute | solution.py:836
  134.4 14.6 %collective-permute-start.4 = (f32[128,1024]{1,0:T(8,128)}, f32[128,1024]{1,0:T(8,128)}, u32[]{:S(2)}, u32[]{:S(2)}) collective-permute-start(f32[128,1024]{1,0:T(8,128)} %slice.143), channel_id=1, source_target_pairs={{0,1},{1,0},{2,3},{3,2},{4,5},{5,4},{6,7},{7,6},{8,9},{9,8},{10,11... | collective-permute-start | bytes 1572872 | tf_op jit(solution)/shard_map/ppermute | solution.py:836
  144.9 37.2 %collective-permute-start.2 = (f32[128,960]{0,1:T(8,128)}, f32[128,960]{0,1:T(8,128)}, u32[]{:S(2)}, u32[]{:S(2)}) collective-permute-start(f32[128,960]{0,1:T(8,128)} %slice.141), channel_id=1, source_target_pairs={{0,1},{1,0},{2,3},{3,2},{4,5},{5,4},{6,7},{7,6},{8,9},{9,8},{10,11... | collective-permute-start | bytes 1474568 | tf_op jit(solution)/shard_map/ppermute | solution.py:836
  173.6 8.6 %copy-start.30 = (f32[960]{0:T(1024)S(1)}, f32[960]{0:T(1024)}, u32[]{:S(2)}) copy-start(f32[960]{0:T(1024)} %param.25) | copy-start | bytes 11524
  173.6 8.6 %copy-start.42 = (f32[128]{0:T(128)S(1)}, f32[128]{0:T(128)}, u32[]{:S(2)}) copy-start(f32[128]{0:T(128)} %copy-done.41) | copy-start | bytes 1540
  173.6 8.6 %copy-start.44 = (f32[128]{0:T(128)S(1)}, f32[128]{0:T(128)}, u32[]{:S(2)}) copy-start(f32[128]{0:T(128)} %copy-done.43) | copy-start | bytes 1540
  173.6 8.6 %copy-start.48 = (f32[128]{0:T(128)S(1)}, f32[128]{0:T(128)}, u32[]{:S(2)}) copy-start(f32[128]{0:T(128)} %copy-done.47) | copy-start | bytes 1540
  178.4 6.7 %collective-permute-start.8 = (bf16[128,960]{0,1:T(8,128)(2,1)}, bf16[128,960]{0,1:T(8,128)(2,1)}, u32[]{:S(2)}, u32[]{:S(2)}) collective-permute-start(bf16[128,960]{0,1:T(8,128)(2,1)} %fusion.89), channel_id=1, source_target_pairs={{0,1},{1,0},{2,3},{3,2},{4,5},{5,4},{6,7},{7,6},{8,9},{9,8},{10,11... | collective-permute-start | bytes 737288 | tf_op jit(solution)/shard_map/ppermute | solution.py:836
  180.5 6.2 %collective-permute-start.6 = (bf16[128,1600]{0,1:T(8,128)(2,1)}, bf16[128,1600]{0,1:T(8,128)(2,1)S(1)}, u32[]{:S(2)}, u32[]{:S(2)}) collective-permute-start(bf16[128,1600]{0,1:T(8,128)(2,1)} %pad_maximum_fusion.6), channel_id=1, source_target_pairs={{0,1},{1,0},{2,3},{3,2},{4,5},{5,4},{6,7},{7,6},{8,9},{9,8},{10,11... | collective-permute-start | bytes 1228808 | tf_op jit(solution)/shard_map/ppermute | solution.py:836
  292.5 6.2 %collective-permute-start.9 = (bf16[32,2560]{1,0:T(8,128)(2,1)S(1)}, bf16[32,2560]{1,0:T(8,128)(2,1)S(1)}, u32[]{:S(2)}, u32[]{:S(2)}) collective-permute-start(bf16[32,2560]{1,0:T(8,128)(2,1)S(1)} %get-tuple-element.43), channel_id=1, source_target_pairs={{0,1},{1,0},{2,3},{3,2},{4,5},{5,4},{6,7},{7,6},{8,9},{9,8},{10,11... | collective-permute-start | bytes 491528 | tf_op jit(solution)/shard_map/ppermute | solution.py:836
  (40 other events, 151.5 us)
